TPU v7x, 256 devices: a whole 4x4x8 slice. The times are simulated.
256 devices in a mesh: ep: 64 (over z_lo, x, y), tp: 4 (over z_hi, core).
Axes of the slice: x: 4, y: 4, z: 8 (z_hi: 2, z_lo: 4; z = z_hi * 4 + z_lo), core: 2. Of those that a mesh axis runs over, the one named last changes fastest.
Arguments:
- activations: float32 [256, 256, 1280], P(('ep', 'tp')), may hold values from -6 to 6
- out_grad: float32 [256, 256, 1280], P(('ep', 'tp')), may hold values from -6 to 6
- slot_out: float32 [256, 128, 1280], P(('ep', 'tp')), may hold values from -6 to 6
- slot_proj: float32 [1280, 128], replicated, may hold values from -1.5625 to 1.5625
- w_in: bfloat16 [64, 1280, 5120], P('ep', None, 'tp'), may hold values from -0.15625 to 0.15625
- w_out: bfloat16 [64, 5120, 1280], P('ep', 'tp'), may hold values from -0.078125 to 0.078125
Outputs:
- d_acts: float32 [256, 256, 1280], P(('ep', 'tp'))
- d_proj: float32 [1280, 128], P('tp', 'ep')
All inputs are finite; a program needn't handle non-finite values.
Results may differ from a plain program's by a relative error of at most 0.0025.
Values may be sent and summed in bfloat16 or wider, within the bound.
A program may use at most 128 MiB of HBM per device.

v0:
```python
import jax
import jax.numpy as jnp
from jax import lax
from jax.sharding import PartitionSpec as P


def gelu_slope(pre_act):
    normal_cdf = 0.5 * (1.0 + lax.erf(pre_act * 0.7071067811865476))
    density = jnp.exp(-0.5 * pre_act * pre_act) * 0.3989422804014327
    return normal_cdf + pre_act * density


def send_back(summed):
    return lax.all_to_all(summed, "ep", split_axis=1, concat_axis=1, tiled=True)


def contract_last(left, right):
    return lax.dot_general(
        left, right, (((1,), (1,)), ((), ())), preferred_element_type=jnp.float32
    )


def local(activations, out_grad, slot_out, slot_proj, w_in, w_out):
    highest = lax.Precision.HIGHEST
    images = activations.shape[0]
    model_width = activations.shape[2]
    slot_count = slot_proj.shape[1]
    ep_count = lax.axis_size("ep")
    tp_count = lax.axis_size("tp")
    logits = jnp.einsum("bmd,dn->bmn", activations, slot_proj, precision=highest)
    dispatch = jax.nn.softmax(logits, axis=1)
    combine = jax.nn.softmax(logits, axis=2)
    slot_in = jnp.einsum("bmn,bmd->bnd", dispatch, activations, precision=highest).astype(
        jnp.bfloat16
    )
    slot_grad = jnp.einsum("bmn,bmd->bnd", combine, out_grad, precision=highest).astype(
        jnp.bfloat16
    )
    grouped = (images, ep_count, slot_count // ep_count, model_width)
    first_proj = w_in[0]
    second_proj = w_out[0]
    recv_in = lax.all_to_all(
        slot_in.reshape(grouped), "ep", split_axis=1, concat_axis=1, tiled=True
    )
    recv_grad = lax.all_to_all(
        slot_grad.reshape(grouped), "ep", split_axis=1, concat_axis=1, tiled=True
    )
    layout = recv_in.shape
    all_in = lax.all_gather(recv_in, "tp", axis=0, tiled=True)
    all_grad = lax.all_gather(recv_grad, "tp", axis=0, tiled=True)
    pre_act = jnp.dot(
        all_in.reshape(-1, model_width), first_proj, preferred_element_type=jnp.float32
    )
    hidden_grad = contract_last(all_grad.reshape(-1, model_width), second_proj)
    pre_grad = (hidden_grad * gelu_slope(pre_act)).astype(jnp.bfloat16)
    summed = lax.psum_scatter(
        contract_last(pre_grad, first_proj), "tp", scatter_dimension=0, tiled=True
    )
    returned = send_back(summed.reshape(layout))
    slot_in_grad = returned.reshape(images, slot_count, model_width)
    comb_grad = jnp.einsum("bmd,bnd->bmn", out_grad, slot_out, precision=highest)
    disp_grad = jnp.einsum("bmd,bnd->bmn", activations, slot_in_grad, precision=highest)
    logit_grad = combine * (comb_grad - jnp.sum(comb_grad * combine, axis=2, keepdims=True))
    logit_grad = logit_grad + dispatch * (
        disp_grad - jnp.sum(disp_grad * dispatch, axis=1, keepdims=True)
    )
    d_acts = jnp.einsum("bmn,bnd->bmd", dispatch, slot_in_grad, precision=highest)
    d_acts = d_acts + jnp.einsum("bmn,dn->bmd", logit_grad, slot_proj, precision=highest)
    proj_term = jnp.einsum("bmd,bmn->dn", activations, logit_grad, precision=highest)
    summed_proj = lax.psum(proj_term, ("ep", "tp"))
    row_count = model_width // tp_count
    col_count = slot_count // ep_count
    d_proj = lax.dynamic_slice(
        summed_proj,
        (lax.axis_index("tp") * row_count, lax.axis_index("ep") * col_count),
        (row_count, col_count),
    )
    return (d_acts, d_proj)


def solution(mesh):
    placed = (
        P(("ep", "tp"), None, None),
        P(("ep", "tp"), None, None),
        P(("ep", "tp"), None, None),
        P(),
        P("ep", None, "tp"),
        P("ep", "tp", None),
    )
    return jax.shard_map(
        local,
        mesh=mesh,
        in_specs=placed,
        out_specs=(P(("ep", "tp"), None, None), P("tp", "ep")),
        check_vma=False,
    )
```

profile of v0, /device:TPU:1, one launch (start us, length us, event | category | flops | bytes accessed | tf_op | source)
XLA Modules:
  0.0 485.2 jit_solution(8092992715231798990)
XLA Ops:
  7.2 2.9 fusion.41
  10.4 1.6 convolution_convert_fusion
  11.9 1.8 reshape.108
  13.7 24.7 %all_to_all.15 = bf16[1,64,2,1280]{3,2,0,1:T(2,128)(2,1)S(1)} all-to-all(bf16[1,64,2,1280]{3,2,0,1:T(2,128)(2,1)} %bitcast.55), channel_id=1, replica_groups=mesh['ep'=64,'tp'=4] {'ep'}, dimensions={1} | all-to-all | bytes 655360 | tf_op jit(solution)/shard_map/all_to_all | solution.py:42
  38.5 0.8 copy.23
  39.3 2.9 convolution_convert_fusion.1
  42.2 1.8 reshape.106
  44.1 24.1 %all_to_all.16 = bf16[1,64,2,1280]{3,2,0,1:T(2,128)(2,1)S(1)} all-to-all(bf16[1,64,2,1280]{3,2,0,1:T(2,128)(2,1)} %bitcast.56), channel_id=1, replica_groups=mesh['ep'=64,'tp'=4] {'ep'}, dimensions={1} | all-to-all | bytes 655360 | tf_op jit(solution)/shard_map/all_to_all | solution.py:45
  68.2 0.8 copy.20
  69.0 0.2 reduce-scatter.2.cloned.1.call-start
  69.2 2.9 all-gather.5.cloned.1.call-done
  72.1 3.7 copy.24
  75.9 4.1 reshape.109
  79.9 31.3 %all-gather.3.cloned.1.call-done = bf16[4,64,2,1280]{3,1,2,0:T(8,128)(2,1)} async-done(((bf16[1,64,2,1280]{3,1,2,0:T(8,128)(2,1)}), bf16[4,64,2,1280]{3,1,2,0:T(8,128)(2,1)}) %all-gather.3.cloned.1.call-update) | async-done | bytes 1310736 | tf_op jit(solution)/shard_map/all_gather | solution.py:50
  111.2 3.7 copy.21
  114.9 4.1 reshape.107
  118.9 4.7 fusion.2
  123.6 8.4 %fusion = f32[512,1280]{1,0:T(8,128)} fusion(bf16[1,1280,1280]{2,1,0:T(8,128)(2,1)S(1)} %copy-done, bf16[512,1280]{1,0:T(8,128)(2,1)} %reshape.107, bf16[1,1280,1280]{2,1,0:T(8,128)(2,1)} %param.11, f32[512,1280]{1,0:T(8,128)} %fusion.2), kind=kOutput, calls=%fused_computation.2 | convolution fusion | flops 3361996800 | bytes 13107200 | tf_op jit(solution)/shard_map/dot_general | solution.py:18
  132.0 59.5 %reduce-scatter.2.cloned.1.call-done = f32[128,1280]{1,0:T(8,128)} async-done(((f32[512,1280]{1,0:T(8,128)}), f32[128,1280]{1,0:T(8,128)}) %reduce-scatter.2.cloned.1.call-update) | async-done | bytes 655376 | tf_op jit(solution)/shard_map/reduce_scatter | solution.py:56
  191.6 2.3 reshape.110
  193.9 7.8 %all-to-all-start.2 = ((f32[1,64,2,1280]{3,2,0,1:T(2,128)}), f32[1,64,2,1280]{3,2,0,1:T(2,128)}, u32[]{:S(2)}, u32[]{:S(2)}) async-start(f32[1,64,2,1280]{3,2,0,1:T(2,128)} %bitcast.54), calls=%async_computation.3 | async-start | bytes 1310720 | tf_op jit(solution)/shard_map/all_to_all | solution.py:14
  201.6 0.3 all-reduce.2.cloned.1.call-start
  201.9 19.0 %all-to-all-done.2 = f32[1,64,2,1280]{3,2,0,1:T(2,128)} async-done(((f32[1,64,2,1280]{3,2,0,1:T(2,128)}), f32[1,64,2,1280]{3,2,0,1:T(2,128)}, u32[]{:S(2)}, u32[]{:S(2)}) %all-to-all-start.2) | async-done | bytes 655392 | tf_op jit(solution)/shard_map/all_to_all | solution.py:14
  220.9 2.4 reshape.111
  223.3 2.8 fusion.22
  226.2 1.3 multiply_reduce_fusion.1
  227.5 0.6 copy-done.5
  228.1 1.8 convolution_bitcast_fusion
  230.0 2.3 fusion.37
  232.3 2.3 fusion.8
  234.7 242.6 %all-reduce.2.cloned.1.call-done = f32[1280,128]{0,1:T(8,128)} async-done(((f32[1280,128]{0,1:T(8,128)}), f32[1280,128]{0,1:T(8,128)}) %all-reduce.2.cloned.1.call-update) | async-done | bytes 655376 | tf_op jit(solution)/shard_map/psum | solution.py:70
  477.3 1.4 dynamic_slice.3
  (30 shorter events, 0.4 us)
Async XLA Ops:
  7.2 111.8 %copy-start = (bf16[1,1280,1280]{2,1,0:T(8,128)(2,1)S(1)}, bf16[1,1280,1280]{2,1,0:T(8,128)(2,1)}, u32[]{:S(2)}) copy-start(bf16[1,1280,1280]{2,1,0:T(8,128)(2,1)} %param.10) | copy-start | bytes 9830404
  7.2 65.0 %all-gather.5.cloned.1.call-start = ((), (), s32[]{:S(2)}) async-start(), calls=%async_computation.5 | async-start | bytes 1638400 | tf_op jit(solution)/shard_map/all_gather | solution.py:49
  7.2 3.1 copy-start.1
  39.3 71.9 %all-gather.3.cloned.1.call-start = ((), (), s32[]{:S(2)}) async-start(), calls=%async_computation.4 | async-start | bytes 1638400 | tf_op jit(solution)/shard_map/all_gather | solution.py:50
  69.0 122.6 %reduce-scatter.2.cloned.1.call-start = ((), (), s32[]{:S(2)}) async-start(), calls=%async_computation.6 | async-start | bytes 3276800 | tf_op jit(solution)/shard_map/reduce_scatter | solution.py:56
  193.9 27.1 %all-to-all-start.2 = ((f32[1,64,2,1280]{3,2,0,1:T(2,128)}), f32[1,64,2,1280]{3,2,0,1:T(2,128)}, u32[]{:S(2)}, u32[]{:S(2)}) async-start(f32[1,64,2,1280]{3,2,0,1:T(2,128)} %bitcast.54), calls=%async_computation.3 | async-start | bytes 1310720 | tf_op jit(solution)/shard_map/all_to_all | solution.py:14
  201.6 275.6 %all-reduce.2.cloned.1.call-start = ((), (), s32[]{:S(2)}) async-start(), calls=%async_computation.7 | async-start | bytes 1310720 | tf_op jit(solution)/shard_map/psum | solution.py:70
  223.3 2.9 copy-start.3
  223.3 2.9 copy-start.7
  226.2 1.9 copy-start.2
  227.4 0.7 copy-start.5
  227.5 0.7 copy-start.8
  227.5 0.6 copy-start.10
  229.9 2.4 copy-start.4
  229.9 2.4 copy-start.6
  229.9 2.4 copy-start.9
  229.9 2.4 copy-start.11
Sparse Core Ops, SparseCore 0:
  39.4 32.7 all-gather.4
  74.0 37.1 all-gather.2
  132.1 59.3 reduce-scatter.1
  230.0 247.1 all-reduce.1
where the time goes:
time: 486 us; the launch traced here: 485 us
  waiting for transfers between devices  355 us (73%)
  blocking collectives  48.8 us (10%)
  matrix products  31 us (6%)
  local copies, waits for them, and re-layouts  27.5 us (6%)
  between operations  13.9 us (3%)
  starting transfers between devices  8.32 us (2%)
    psum x1, waiting for transfers between devices, local(): summed_proj = lax.psum(proj_term, ('ep', 'tp'))  243 us
    reduce_scatter x1, waiting for transfers between devices, local(): lax.psum_scatter(contract_last(pre_grad, first_proj), 'tp', scatter_dimen...  59.5 us
    all_gather x1, waiting for transfers between devices, local(): all_grad = lax.all_gather(recv_grad, 'tp', axis=0, tiled=True)  31.3 us
    all_to_all x1, blocking collectives, local(): lax.all_to_all(slot_in.reshape(grouped), 'ep', split_axis=1, concat_axis=...  24.7 us
    all_to_all x1, blocking collectives, local(): lax.all_to_all(slot_grad.reshape(grouped), 'ep', split_axis=1, concat_axi...  24.1 us
    all_to_all x1, waiting for transfers between devices, send_back(): return lax.all_to_all(summed, 'ep', split_axis=1, concat_axis=1, tiled=True)  19 us
  transfers between devices with their start and end apart: 5, of which 5 were waited for; matrix products, arithmetic and copies ran while one was open for 4% of the time, Pallas kernels for 0%

commit v1 on v0

--- a/solution.py
+++ b/solution.py
@@ -66,15 +66,20 @@
     )
     d_acts = jnp.einsum("bmn,bnd->bmd", dispatch, slot_in_grad, precision=highest)
     d_acts = d_acts + jnp.einsum("bmn,dn->bmd", logit_grad, slot_proj, precision=highest)
-    proj_term = jnp.einsum("bmd,bmn->dn", activations, logit_grad, precision=highest)
-    summed_proj = lax.psum(proj_term, ("ep", "tp"))
+    proj_term = jnp.einsum("bmn,bmd->nd", logit_grad, activations, precision=highest)
     row_count = model_width // tp_count
     col_count = slot_count // ep_count
+    parts = lax.all_to_all(
+        proj_term.reshape(ep_count, col_count, model_width),
+        "ep",
+        split_axis=0,
+        concat_axis=0,
+        tiled=True,
+    )
+    summed_proj = lax.psum(jnp.sum(parts, axis=0), "tp")
     d_proj = lax.dynamic_slice(
-        summed_proj,
-        (lax.axis_index("tp") * row_count, lax.axis_index("ep") * col_count),
-        (row_count, col_count),
-    )
+        summed_proj, (0, lax.axis_index("tp") * row_count), (col_count, row_count)
+    ).T
     return (d_acts, d_proj)
 
 

time: 486 us -> 287 us (0.59)
  waiting for transfers between devices: 355 us -> 107 us
  blocking collectives: 48.8 us -> 92.7 us
    psum x1 -> x0, waiting for transfers between devices: 243 us -> none  [local(): summed_proj = lax.psum(proj_term, ('ep', 'tp'))]
    all_to_all x0 -> x1, blocking collectives: none -> 27 us  [send_back(): return lax.all_to_all(summed, 'ep', split_axis=1, concat_axis=1, tiled=True)]
    psum x0 -> x1, blocking collectives: none -> 17.2 us  [local(): summed_proj = lax.psum(jnp.sum(parts, axis=0), 'tp')]
    all_to_all x1, waiting for transfers between devices: 19 us -> 13.2 us  [local(): lax.all_to_all(proj_term.reshape(ep_count, col_count, model_width), 'ep',...]
  transfers between devices with their start and end apart: 5 -> 4, of which waited for: 5 -> 4; matrix products, arithmetic and copies ran while one was open for 4% -> 7% of each run, Pallas kernels for 0% -> 0%
where the time goes in v1:
time: 287 us; the launch traced here: 285 us
  waiting for transfers between devices  107 us (37%)
  blocking collectives  92.7 us (32%)
  matrix products  32.7 us (11%)
  local copies, waits for them, and re-layouts  29.7 us (10%)
  between operations  13.9 us (5%)
  starting transfers between devices  5.99 us (2%)
    reduce_scatter x1, waiting for transfers between devices, local(): lax.psum_scatter(contract_last(pre_grad, first_proj), 'tp', scatter_dimen...  59.5 us
    all_gather x1, waiting for transfers between devices, local(): all_grad = lax.all_gather(recv_grad, 'tp', axis=0, tiled=True)  31.3 us
    all_to_all x1, blocking collectives, send_back(): return lax.all_to_all(summed, 'ep', split_axis=1, concat_axis=1, tiled=True)  27 us
    all_to_all x1, blocking collectives, local(): lax.all_to_all(slot_in.reshape(grouped), 'ep', split_axis=1, concat_axis=...  24.7 us
    all_to_all x1, blocking collectives, local(): lax.all_to_all(slot_grad.reshape(grouped), 'ep', split_axis=1, concat_axi...  23.7 us
    psum x1, blocking collectives, local(): summed_proj = lax.psum(jnp.sum(parts, axis=0), 'tp')  17.2 us
    all_to_all x1, waiting for transfers between devices, local(): lax.all_to_all(proj_term.reshape(ep_count, col_count, model_width), 'ep',...  13.2 us
    dot_general x1, matrix products, contract_last(): lax.dot_general(left, right, (((1,), (1,)), ((), ())), preferred_element_...  8.39 us
  transfers between devices with their start and end apart: 4, of which 4 were waited for; matrix products, arithmetic and copies ran while one was open for 7% of the time, Pallas kernels for 0%

profile of v1, /device:TPU:1, one launch (start us, length us, event | category | flops | bytes accessed | tf_op | source)
XLA Modules:
  0.0 284.6 jit_solution(289200511458709398)
XLA Ops:
  7.2 2.9 %fusion.48 = (f32[128]{0:T(128)S(1)}, f32[256]{0:T(256)S(1)}, f32[256,128]{0,1:T(8,128)S(1)}) fusion(f32[1280,128]{1,0:T(8,128)} %param.9, f32[1,256,1280]{2,1,0:T(8,128)} %param.6), kind=kOutput, calls=%fused_computation.51 | convolution fusion | flops 503381632 | bytes 2098688 | tf_op jit(solution)/shard_map/bmd,dn->bmn/dot_general | solution.py:30
  10.4 1.6 convolution_convert_fusion
  11.9 1.8 reshape.110
  13.7 24.7 %all_to_all.20 = bf16[1,64,2,1280]{3,2,0,1:T(2,128)(2,1)S(1)} all-to-all(bf16[1,64,2,1280]{3,2,0,1:T(2,128)(2,1)} %bitcast.68), channel_id=1, replica_groups=mesh['ep'=64,'tp'=4] {'ep'}, dimensions={1} | all-to-all | bytes 655360 | tf_op jit(solution)/shard_map/all_to_all | solution.py:42
  39.3 2.9 %convolution_convert_fusion.1 = bf16[128,1280]{1,0:T(8,128)(2,1)} fusion(f32[1,256,1280]{2,1,0:T(8,128)} %param.7, f32[256,128]{0,1:T(8,128)S(1)} %get-tuple-element.8, f32[256]{0:T(256)S(1)} %get-tuple-element.5, f32[256]{0:T(256)S(1)} %get-tuple-element.7), kind=kOutput, calls=%fused_computation.15 | convolution fusion | flops 503545856 | bytes 1771520 | tf_op jit(solution)/shard_map/bmn,bmd->bnd/dot_general | solution.py:36
  42.1 1.8 reshape.108
  44.0 23.7 %all_to_all.21 = bf16[1,64,2,1280]{3,2,0,1:T(2,128)(2,1)S(1)} all-to-all(bf16[1,64,2,1280]{3,2,0,1:T(2,128)(2,1)} %bitcast.69), channel_id=1, replica_groups=mesh['ep'=64,'tp'=4] {'ep'}, dimensions={1} | all-to-all | bytes 655360 | tf_op jit(solution)/shard_map/all_to_all | solution.py:45
  67.7 0.8 copy.17
  68.7 3.3 %all-gather.5.cloned.1.call-done = bf16[4,64,2,1280]{3,1,2,0:T(8,128)(2,1)} async-done(((bf16[1,64,2,1280]{3,1,2,0:T(8,128)(2,1)}), bf16[4,64,2,1280]{3,1,2,0:T(8,128)(2,1)}) %all-gather.5.cloned.1.call-update) | async-done | bytes 1310736 | tf_op jit(solution)/shard_map/all_gather | solution.py:49
  72.0 3.7 %copy.21 = bf16[4,64,2,1280]{3,2,1,0:T(2,128)(2,1)} copy(bf16[4,64,2,1280]{3,1,2,0:T(8,128)(2,1)} %all-gather.5.cloned.1.call-done) | data formatting | bytes 2621440 | tf_op jit(solution)/shard_map/all_gather | solution.py:49
  75.8 4.1 %reshape.111 = bf16[512,1280]{1,0:T(8,128)(2,1)} reshape(bf16[4,64,2,1280]{3,2,1,0:T(2,128)(2,1)} %copy.21) | data formatting | bytes 2621440 | tf_op jit(solution)/shard_map/reshape | solution.py:52
  79.8 31.3 %all-gather.3.cloned.1.call-done = bf16[4,64,2,1280]{3,1,2,0:T(8,128)(2,1)} async-done(((bf16[1,64,2,1280]{3,1,2,0:T(8,128)(2,1)}), bf16[4,64,2,1280]{3,1,2,0:T(8,128)(2,1)}) %all-gather.3.cloned.1.call-update) | async-done | bytes 1310736 | tf_op jit(solution)/shard_map/all_gather | solution.py:50
  111.1 3.7 %copy.18 = bf16[4,64,2,1280]{3,2,1,0:T(2,128)(2,1)} copy(bf16[4,64,2,1280]{3,1,2,0:T(8,128)(2,1)} %all-gather.3.cloned.1.call-done) | data formatting | bytes 2621440 | tf_op jit(solution)/shard_map/all_gather | solution.py:50
  114.8 4.1 %reshape.109 = bf16[512,1280]{1,0:T(8,128)(2,1)} reshape(bf16[4,64,2,1280]{3,2,1,0:T(2,128)(2,1)} %copy.18) | data formatting | bytes 2621440 | tf_op jit(solution)/shard_map/reshape | solution.py:54
  118.9 4.7 %fusion.2 = f32[512,1280]{1,0:T(8,128)} fusion(bf16[512,1280]{1,0:T(8,128)(2,1)} %reshape.111, bf16[1,1280,1280]{2,1,0:T(8,128)(2,1)S(1)} %copy-done), kind=kOutput, calls=%fused_computation.4 | convolution fusion | flops 1677721600 | bytes 7208960 | tf_op jit(solution)/shard_map/dot_general | solution.py:51
  123.6 8.4 %fusion = f32[512,1280]{1,0:T(8,128)} fusion(bf16[1,1280,1280]{2,1,0:T(8,128)(2,1)S(1)} %copy-done, bf16[512,1280]{1,0:T(8,128)(2,1)} %reshape.109, bf16[1,1280,1280]{2,1,0:T(8,128)(2,1)} %param.11, f32[512,1280]{1,0:T(8,128)} %fusion.2), kind=kOutput, calls=%fused_computation.2 | convolution fusion | flops 3361996800 | bytes 13107200 | tf_op jit(solution)/shard_map/dot_general | solution.py:18
  132.0 59.5 %reduce-scatter.2.cloned.1.call-done = f32[128,1280]{1,0:T(8,128)} async-done(((f32[512,1280]{1,0:T(8,128)}), f32[128,1280]{1,0:T(8,128)}) %reduce-scatter.2.cloned.1.call-update) | async-done | bytes 655376 | tf_op jit(solution)/shard_map/reduce_scatter | solution.py:56
  191.5 2.3 reshape.112
  193.8 27.0 %all_to_all.22 = f32[1,64,2,1280]{3,2,0,1:T(2,128)} all-to-all(f32[1,64,2,1280]{3,2,0,1:T(2,128)} %bitcast.67), channel_id=1, replica_groups=mesh['ep'=64,'tp'=4] {'ep'}, dimensions={1} | all-to-all | bytes 1310720 | tf_op jit(solution)/shard_map/all_to_all | solution.py:14
  220.9 2.4 reshape.113
  223.3 3.1 %fusion.18 = f32[128,256]{1,0:T(8,128)S(1)} fusion(f32[128,1280]{1,0:T(8,128)} %reshape.113, f32[1,256,1280]{2,1,0:T(8,128)} %param.6), kind=kOutput, calls=%fused_computation.21 | convolution fusion | flops 503316480 | bytes 2097152 | tf_op jit(solution)/shard_map/bmd,bnd->bmn/dot_general | solution.py:62
  226.4 1.5 multiply_reduce_fusion
  228.5 0.8 fusion.26
  229.2 1.6 dot_general.48
  230.9 2.2 fusion.13
  233.1 1.4 copy.24
  234.4 5.7 %all-to-all-start.3 = ((f32[64,2,1280]{2,1,0:T(2,128)}), f32[64,2,1280]{2,1,0:T(2,128)}, u32[]{:S(2)}, u32[]{:S(2)}) async-start(f32[64,2,1280]{2,1,0:T(2,128)} %copy.24), calls=%async_computation.4 | async-start | bytes 1310720 | tf_op jit(solution)/shard_map/all_to_all | solution.py:72
  240.2 2.5 fusion.45
  242.7 3.1 %fusion.8 = f32[1,256,1280]{2,1,0:T(8,128)} fusion(f32[256,1280]{1,0:T(8,128)S(1)} %fusion.45, f32[1280,128]{1,0:T(8,128)S(1)} %copy-done.3, f32[128,256]{1,0:T(8,128)S(1)} %fusion.18, f32[128]{0:T(128)} %copy-done.8, f32[256,128]{0,1:T(8,128)S(1)} %copy-done.5, f32[256]{0:T(256)} %copy-done.7, f32[256,128]{0,1:T(8,128)S(1)} %get-tuple-element.8, ...), kind=kOutput, calls=%fused_computation.9 | convolution fusion | flops 503939072 | bytes 3674624 | tf_op jit(solution)/shard_map/bmn,dn->bmd/dot_general | solution.py:68
  245.7 13.2 %all-to-all-done.3 = f32[64,2,1280]{2,1,0:T(2,128)} async-done(((f32[64,2,1280]{2,1,0:T(2,128)}), f32[64,2,1280]{2,1,0:T(2,128)}, u32[]{:S(2)}, u32[]{:S(2)}) %all-to-all-start.3) | async-done | bytes 655392 | tf_op jit(solution)/shard_map/all_to_all | solution.py:72
  258.9 1.3 reduce_sum.49
  260.2 17.2 %psum.7 = f32[2,1280]{1,0:T(2,128)S(1)} all-reduce(f32[2,1280]{1,0:T(2,128)S(1)} %reduce_sum.49), channel_id=1, replica_groups=mesh['ep'=64,'tp'=4] {'tp'}, use_global_device_ids=true, to_apply=%region_8.0 | all-reduce | flops 2560 | bytes 20480 | tf_op jit(solution)/shard_map/psum | solution.py:79
  (27 shorter events, 2.6 us)
Async XLA Ops:
  7.2 111.7 %copy-start = (bf16[1,1280,1280]{2,1,0:T(8,128)(2,1)S(1)}, bf16[1,1280,1280]{2,1,0:T(8,128)(2,1)}, u32[]{:S(2)}) copy-start(bf16[1,1280,1280]{2,1,0:T(8,128)(2,1)} %param.10) | copy-start | bytes 9830404
  7.2 64.9 %all-gather.5.cloned.1.call-start = ((), (), s32[]{:S(2)}) async-start(), calls=%async_computation.6 | async-start | bytes 1638400 | tf_op jit(solution)/shard_map/all_gather | solution.py:49
  7.2 3.1 %copy-start.1 = (f32[1,256,1280]{2,1,0:T(8,128)S(1)}, f32[1,256,1280]{2,1,0:T(8,128)}, u32[]{:S(2)}) copy-start(f32[1,256,1280]{2,1,0:T(8,128)} %param.6) | copy-start | bytes 3932164
  39.2 71.9 %all-gather.3.cloned.1.call-start = ((), (), s32[]{:S(2)}) async-start(), calls=%async_computation.5 | async-start | bytes 1638400 | tf_op jit(solution)/shard_map/all_gather | solution.py:50
  68.5 123.1 %reduce-scatter.2.cloned.1.call-start = ((), (), s32[]{:S(2)}) async-start(), calls=%async_computation.7 | async-start | bytes 3276800 | tf_op jit(solution)/shard_map/reduce_scatter | solution.py:56
  223.3 3.1 %copy-start.2 = (f32[1,256,1280]{2,1,0:T(8,128)S(1)}, f32[1,256,1280]{2,1,0:T(8,128)}, u32[]{:S(2)}) copy-start(f32[1,256,1280]{2,1,0:T(8,128)} %param.7) | copy-start | bytes 3932164
  223.3 3.1 %copy-start.6 = (f32[1,128,1280]{2,1,0:T(8,128)S(1)}, f32[1,128,1280]{2,1,0:T(8,128)}, u32[]{:S(2)}) copy-start(f32[1,128,1280]{2,1,0:T(8,128)} %param.8) | copy-start | bytes 1966084
  227.8 0.6 copy-start.4
  227.8 0.6 copy-start.7
  227.9 0.6 copy-start.8
  234.4 24.5 %all-to-all-start.3 = ((f32[64,2,1280]{2,1,0:T(2,128)}), f32[64,2,1280]{2,1,0:T(2,128)}, u32[]{:S(2)}, u32[]{:S(2)}) async-start(f32[64,2,1280]{2,1,0:T(2,128)} %copy.24), calls=%async_computation.4 | async-start | bytes 1310720 | tf_op jit(solution)/shard_map/all_to_all | solution.py:72
  240.1 2.5 copy-start.3
  240.1 2.5 copy-start.5
Sparse Core Ops, SparseCore 0:
  39.3 32.6 all-gather.4
  73.8 37.2 all-gather.2
  132.1 59.3 reduce-scatter.1

commit v2 on v0

v2 whole, which is shorter than its diff:
```python
import functools

import jax
import jax.numpy as jnp
from jax import lax
from jax.experimental import pallas as pl
from jax.experimental.pallas import tpu as pltpu
from jax.sharding import PartitionSpec as P

MESH = pl.DeviceIdType.MESH
F32 = jnp.float32
BF16 = jnp.bfloat16
D = 1280
HALF = 640
TOKENS = 256
SLOTS = 128
ROWS = 256
PLANE = 16
RING = 8
FORWARD = (
    (0, 0, 128), (0, 128, 256), (0, 384, 256),
    (1, 0, 256), (1, 256, 256), (1, 512, 128),
)
BACK = ((0, 256), (256, 256), (512, 256), (768, 256), (1024, 256))
NF, NB = len(FORWARD), len(BACK)


def gelu_slope(pre_act):
    normal_cdf = 0.5 * (1.0 + lax.erf(pre_act * 0.7071067811865476))
    density = jnp.exp(-0.5 * pre_act * pre_act) * 0.3989422804014327
    return normal_cdf + pre_act * density


def dot_nn(a, b):
    return jnp.dot(a, b, preferred_element_type=F32)


def dot_nt(a, b):
    return lax.dot_general(a, b, (((1,), (1,)), ((), ())), preferred_element_type=F32)


def split(a):
    high = a.astype(BF16)
    return high, (a - high.astype(F32)).astype(BF16)


def three(dot, a, b):
    return dot(a[0], b[0]) + (dot(a[0], b[1]) + dot(a[1], b[0]))


def iota2(shape, axis):
    return lax.broadcasted_iota(jnp.int32, shape, axis)


def one_hot(condition):
    return jnp.where(condition, 1.0, 0.0).astype(BF16)


def kernel(
    acts_hbm, og_hbm, so_hbm, sp_hbm, wi_hbm, wo_hbm,
    dacts_hbm, dproj_ref,
    acts, og, so, sp, wi, wo,
    acts_s, og_s, so_s, sp_s, disp_s, comb, disp, comb_term, disp_grad, dacts,
    send, plane_in, ring_out, ring_in, other_in,
    acc, pre_grad, part, part_in, back_out, back_in, back_send, sig,
    dp, dp_in, dp_sum, dp_plane, dp_ring, dp_back,
    load_sem, fps, fpr, fzs, fzr, fcs, fcr, bcs, bcr, bzs, bzr, bps, bpr, dps, dpr, out_sem,
):
    ep, tp = lax.axis_index("ep"), lax.axis_index("tp")
    z_lo, pos = lax.div(ep, 16), lax.rem(ep, 16)
    x, y = lax.div(pos, 4), lax.rem(pos, 4)
    z_hi, core = lax.div(tp, 2), lax.rem(tp, 2)
    z = z_hi * 4 + z_lo
    other = {"ep": ep, "tp": z_hi * 2 + (1 - core)}

    def plane_peer(q):
        there = lax.rem(x + lax.div(q, 4), 4) * 4 + lax.rem(y + lax.rem(q, 4), 4)
        return there, {"ep": z_lo * 16 + there, "tp": tp}

    def ring_peer(q):
        there = lax.rem(z + q, RING)
        lo = lax.rem(there, 4)
        return there, lo, {"ep": lo * 16 + pos, "tp": lax.div(there, 4) * 2 + core}

    def remote(src, dst, send_sem, recv_sem, device):
        return pltpu.make_async_remote_copy(
            src_ref=src, dst_ref=dst, send_sem=send_sem, recv_sem=recv_sem,
            device_id=device, device_id_type=MESH,
        )

    def wait_bytes(ref, sem):
        pltpu.make_async_copy(ref, ref, sem).wait()

    loads = []
    pairs = ((sp_hbm, sp), (acts_hbm, acts), (og_hbm, og), (so_hbm, so), (wi_hbm, wi), (wo_hbm, wo))
    for k, (src, dst) in enumerate(pairs):
        loads.append(pltpu.make_async_copy(src, dst, load_sem.at[k]))
        loads[-1].start()
    load_sp, load_acts, load_og, load_so, load_wi, load_wo = loads

    barrier = pltpu.get_barrier_semaphore()

    def greet_plane(q, carry):
        pl.semaphore_signal(barrier, inc=1, device_id=plane_peer(q)[1], device_id_type=MESH)
        return carry

    def greet_ring(q, carry):
        pl.semaphore_signal(barrier, inc=1, device_id=ring_peer(q)[2], device_id_type=MESH)
        return carry

    lax.fori_loop(1, PLANE, greet_plane, 0)
    lax.fori_loop(1, RING, greet_ring, 0)
    pl.semaphore_signal(barrier, inc=1, device_id=other, device_id_type=MESH)

    n, r = iota2((SLOTS, SLOTS), 0), iota2((SLOTS, SLOTS), 1)
    natural = lax.rem(lax.div(r, 2), 4) * 32 + lax.div(r, 8) * 2 + lax.rem(r, 2)
    to_order = one_hot(n == natural)
    natural_t = lax.rem(lax.div(n, 2), 4) * 32 + lax.div(n, 8) * 2 + lax.rem(n, 2)
    to_order_t = one_hot(r == natural_t)
    o, i = iota2((ROWS, ROWS), 0), iota2((ROWS, ROWS), 1)
    source = (
        lax.rem(lax.div(o, 2), 16) * 16 + lax.rem(lax.div(o, 32), 2) * 8
        + lax.div(o, 64) * 2 + lax.rem(o, 2)
    )
    regroup = one_hot(i == source)
    o, i = iota2((SLOTS, ROWS), 0), iota2((SLOTS, ROWS), 1)
    source = lax.rem(lax.div(o, 2), 4) * 32 + lax.div(o, 8) * 2 + lax.rem(o, 2)
    collect = one_hot(lax.rem(i, 128) == source)

    load_sp.wait()
    for k, part_of in enumerate(split(sp[...])):
        sp_s[k] = dot_nn(part_of, to_order).astype(BF16)
    load_acts.wait()
    acts_s[0], acts_s[1] = split(acts[...])
    logits = three(dot_nn, (acts_s[0], acts_s[1]), (sp_s[0], sp_s[1]))
    e = jnp.exp(logits - jnp.max(logits, axis=0, keepdims=True))
    dispatch = e / jnp.sum(e, axis=0, keepdims=True)
    disp[...] = dispatch
    disp_s[0], disp_s[1] = split(dispatch)
    e = jnp.exp(logits - jnp.max(logits, axis=1, keepdims=True))
    combine = e / jnp.sum(e, axis=1, keepdims=True)
    comb[...] = combine

    def slot_rows(kind, weights_t, values, col, width):
        halves = []
        for h in range(2):
            c = h * HALF + col
            rows = three(
                dot_nn, weights_t, (values[0, :, c : c + width], values[1, :, c : c + width])
            )
            halves.append(rows.reshape(PLANE, 8, width))
        both = jnp.concatenate(halves, axis=1).reshape(ROWS, width)
        send[kind, :, col : col + width] = both.astype(BF16)

    def plane_send(k):
        kind, col, width = FORWARD[k]

        def one(q, carry):
            there, device = plane_peer(q)
            remote(
                send.at[kind, pl.ds(there * 16, 16), pl.ds(col, width)],
                plane_in.at[kind, pl.ds(pos * 16, 16), pl.ds(col, width)],
                fps.at[k], fpr.at[k], device,
            ).start()
            return carry

        lax.fori_loop(1, PLANE, one, 0)
        plane_in[kind, pl.ds(pos * 16, 16), pl.ds(col, width)] = send[
            kind, pl.ds(pos * 16, 16), pl.ds(col, width)
        ]

    dispatch_t = split(dispatch.T)
    for k in range(NF):
        kind, col, width = FORWARD[k]
        if kind == 0:
            slot_rows(0, dispatch_t, acts_s, col, width)
            if k == 0:
                pl.semaphore_wait(barrier, PLANE - 1 + RING - 1 + 1)
            plane_send(k)

    load_og.wait()
    og_s[0], og_s[1] = split(og[...])
    combine_t = split(combine.T)
    for k in range(NF):
        kind, col, width = FORWARD[k]
        if kind == 1:
            slot_rows(1, combine_t, og_s, col, width)
            plane_send(k)

    for k in range(NF):
        kind, col, width = FORWARD[k]
        wait_bytes(plane_in.at[kind, pl.ds(0, 240), pl.ds(col, width)], fpr.at[k])
        moved = dot_nn(regroup, plane_in[kind, :, col : col + width])
        ring_out[kind, :, :, col : col + width] = moved.astype(BF16).reshape(8, 32, width)

        def one(q, carry):
            there, lo, device = ring_peer(q)
            remote(
                ring_out.at[kind, pl.ds(lo * 2, 2), :, pl.ds(col, width)],
                ring_in.at[kind, :, pl.ds(z * 32, 32), pl.ds(col, width)],
                fzs.at[k], fzr.at[k], device,
            ).start()
            return carry

        lax.fori_loop(1, RING, one, 0)
        ring_in[kind, :, pl.ds(z * 32, 32), pl.ds(col, width)] = ring_out[
            kind, pl.ds(z_lo * 2, 2), :, pl.ds(col, width)
        ]

    load_so.wait()
    for k, part_of in enumerate(split(so[...])):
        so_s[k] = dot_nn(to_order_t, part_of).astype(BF16)
    comb_grad = three(dot_nt, (og_s[0], og_s[1]), (so_s[0], so_s[1]))
    combine = comb[...]
    comb_term[...] = combine * (
        comb_grad - jnp.sum(comb_grad * combine, axis=1, keepdims=True)
    )

    load_wi.wait()
    load_wo.wait()

    def expert(k, rows_ref, own):
        kind, col, width = FORWARD[k]
        last = k == NF - 1

        def tile(t, carry):
            c = pl.multiple_of(t * 256, 256)
            total = None
            for h in range(2):
                rows = rows_ref[kind, h, :, col : col + width]
                d = h * HALF + col
                if kind == 0:
                    term = dot_nn(rows, wi[pl.ds(d, width), pl.ds(c, 256)])
                else:
                    term = dot_nt(rows, wo[pl.ds(c, 256), pl.ds(d, width)])
                total = term if total is None else total + term
            if col > 0:
                total = total + acc[kind, own, :, pl.ds(c, 256)]
            if kind == 0 and col + width == HALF:
                total = gelu_slope(total)
            if last:
                slope = acc[0, own, :, pl.ds(c, 256)]
                pre_grad[own, :, pl.ds(c, 256)] = (total * slope).astype(BF16)
            else:
                acc[kind, own, :, pl.ds(c, 256)] = total
            return carry

        lax.fori_loop(0, 5, tile, 0)

    for k in range(NF):
        kind, col, width = FORWARD[k]
        wait_bytes(ring_in.at[kind, :, pl.ds(0, 224), pl.ds(col, width)], fzr.at[k])
        across = remote(
            ring_in.at[kind, :, :, pl.ds(col, width)],
            other_in.at[kind, :, :, pl.ds(col, width)],
            fcs.at[k], fcr.at[k], other,
        )
        across.start()
        expert(k, ring_in, 0)
        across.wait_recv()
        expert(k, other_in, 1)

    def back_across(b):
        col, width = BACK[b]
        return remote(
            part.at[1, :, pl.ds(col, width)], part_in.at[:, pl.ds(col, width)],
            bcs.at[b], bcr.at[b], other,
        )

    def back_ring(b):
        col, width = BACK[b]
        back_across(b).wait_recv()
        both = part[0, :, col : col + width] + part_in[:, col : col + width]
        back_out[:, col : col + width] = both.astype(BF16)

        def one(q, carry):
            there, _, device = ring_peer(q)
            remote(
                back_out.at[pl.ds(there * 32, 32), pl.ds(col, width)],
                back_in.at[pl.ds(z * 32, 32), pl.ds(col, width)],
                bzs.at[b], bzr.at[b], device,
            ).start()
            return carry

        lax.fori_loop(1, RING, one, 0)
        back_in[pl.ds(z * 32, 32), pl.ds(col, width)] = back_out[
            pl.ds(z * 32, 32), pl.ds(col, width)
        ]

    for b in range(NB):
        col, width = BACK[b]
        part[1, :, col : col + width] = dot_nt(pre_grad[1], wi[col : col + width, :])
        back_across(b).start()
        part[0, :, col : col + width] = dot_nt(pre_grad[0], wi[col : col + width, :])
        if b > 0:
            back_ring(b - 1)
    back_ring(NB - 1)

    def back_plane(b):
        col, width = BACK[b]
        wait_bytes(back_in.at[pl.ds(0, 224), pl.ds(col, width)], bzr.at[b])
        back_send[:, col : col + width] = dot_nn(collect, back_in[:, col : col + width])

        def one(q, carry):
            there, device = plane_peer(q)
            remote(
                back_send.at[pl.ds(there * 8, 8), pl.ds(col, width)],
                sig.at[pl.ds(pos * 8, 8), pl.ds(col, width)],
                bps.at[b], bpr.at[b], device,
            ).start()
            return carry

        lax.fori_loop(1, PLANE, one, 0)
        sig[pl.ds(pos * 8, 8), pl.ds(col, width)] = back_send[
            pl.ds(pos * 8, 8), pl.ds(col, width)
        ]

    def arrived(b):
        col, width = BACK[b]
        wait_bytes(sig.at[pl.ds(0, 120), pl.ds(col, width)], bpr.at[b])
        grad = split(sig[:, col : col + width])
        tokens = (acts_s[0, :, col : col + width], acts_s[1, :, col : col + width])
        term = three(dot_nt, tokens, grad)
        if b == 0:
            disp_grad[...] = term
        else:
            disp_grad[...] += term
        dacts[:, col : col + width] = three(dot_nn, (disp_s[0], disp_s[1]), grad)

    for b in range(NB):
        back_plane(b)
        if b > 0:
            arrived(b - 1)
    arrived(NB - 1)

    dispatch = disp[...]
    grad = disp_grad[...]
    logit_grad = comb_term[...] + dispatch * (
        grad - jnp.sum(grad * dispatch, axis=0, keepdims=True)
    )
    grad_s = split(logit_grad)
    grad_t = split(logit_grad.T)
    for b in range(NB):
        col, width = BACK[b]
        dp[:, col : col + width] = three(
            dot_nn, grad_t, (acts_s[0, :, col : col + width], acts_s[1, :, col : col + width])
        )

    for k in range(2):
        remote(
            dp.at[:, pl.ds(pl.multiple_of(k * HALF + (1 - core) * 256, 128), 384)],
            dp_in.at[:, pl.ds(k * 384, 384)],
            dps.at[k], dpr.at[k], other,
        ).start()
    for b in range(NB):
        col, width = BACK[b]
        dacts[:, col : col + width] += three(
            dot_nt, grad_s, (sp_s[0, col : col + width, :], sp_s[1, col : col + width, :])
        )
    store = pltpu.make_async_copy(dacts, dacts_hbm, out_sem)
    store.start()
    for k in range(2):
        cols = pl.ds(pl.multiple_of(k * HALF + core * 256, 128), 384)
        wait_bytes(dp_in.at[:, pl.ds(k * 384, 384)], dpr.at[k])
        dp_sum[:, k * 384 : k * 384 + 384] = (
            dp[:, cols] + dp_in[:, k * 384 : k * 384 + 384]
        )

    def proj_plane(q, carry):
        there, device = plane_peer(q)
        remote(
            dp_sum.at[pl.ds(there * 8, 8)], dp_plane.at[pl.ds(pos * 8, 8)],
            dps.at[2], dpr.at[2], device,
        ).start()
        return carry

    lax.fori_loop(1, PLANE, proj_plane, 0)
    dp_plane[pl.ds(pos * 8, 8)] = dp_sum[pl.ds(pos * 8, 8)]
    wait_bytes(dp_plane.at[pl.ds(0, 120)], dpr.at[2])
    dp_ring[...] = jnp.sum(dp_plane[...].reshape(PLANE, 8, 768), axis=0)

    def proj_ring(q, carry):
        there, _, device = ring_peer(q)
        remote(
            dp_ring.at[:, pl.ds(pl.multiple_of(lax.div(there, 4) * 384, 128), 384)],
            dp_back.at[pl.ds(z * 8, 8)],
            dps.at[3], dpr.at[3], device,
        ).start()
        return carry

    lax.fori_loop(1, RING, proj_ring, 0)
    dp_back[pl.ds(z * 8, 8)] = dp_ring[:, pl.ds(pl.multiple_of(z_hi * 384, 128), 384)]
    wait_bytes(dp_back.at[pl.ds(0, 56)], dpr.at[3])
    total = jnp.sum(dp_back[...].reshape(RING, 8, 384), axis=0)
    mine = jnp.where(z_lo == 0, total[0:2], 0.0)
    for k in range(1, 4):
        mine = mine + jnp.where(z_lo == k, total[2 * k : 2 * k + 2], 0.0)
    dproj_ref[...] = jnp.where(core == 0, mine[:, 0:320], mine[:, 64:384])

    for k in range(NF):
        kind, col, width = FORWARD[k]
        wait_bytes(plane_in.at[kind, pl.ds(0, 240), pl.ds(col, width)], fps.at[k])
        wait_bytes(ring_in.at[kind, :, pl.ds(0, 224), pl.ds(col, width)], fzs.at[k])
        wait_bytes(ring_in.at[kind, :, :, pl.ds(col, width)], fcs.at[k])
    for b in range(NB):
        col, width = BACK[b]
        wait_bytes(part_in.at[:, pl.ds(col, width)], bcs.at[b])
        wait_bytes(back_in.at[pl.ds(0, 224), pl.ds(col, width)], bzs.at[b])
        wait_bytes(sig.at[pl.ds(0, 120), pl.ds(col, width)], bps.at[b])
    for k in range(2):
        wait_bytes(dp_in.at[:, pl.ds(k * 384, 384)], dps.at[k])
    wait_bytes(dp_plane.at[pl.ds(0, 120)], dps.at[2])
    wait_bytes(dp_back.at[pl.ds(0, 56)], dps.at[3])
    store.wait()


def local(activations, out_grad, slot_out, slot_proj, w_in, w_out):
    vmem = pltpu.VMEM
    sems = pltpu.SemaphoreType.DMA
    any_space = pl.BlockSpec(memory_space=pl.ANY)
    d_acts, d_proj = pl.pallas_call(
        kernel,
        out_shape=(
            jax.ShapeDtypeStruct((TOKENS, D), F32),
            jax.ShapeDtypeStruct((2, 320), F32),
        ),
        in_specs=[any_space] * 6,
        out_specs=(any_space, pl.BlockSpec(memory_space=pltpu.VMEM)),
        scratch_shapes=[
            vmem((TOKENS, D), F32),
            vmem((TOKENS, D), F32),
            vmem((SLOTS, D), F32),
            vmem((D, SLOTS), F32),
            vmem((D, D), BF16),
            vmem((D, D), BF16),
            vmem((2, TOKENS, D), BF16),
            vmem((2, TOKENS, D), BF16),
            vmem((2, SLOTS, D), BF16),
            vmem((2, D, SLOTS), BF16),
            vmem((2, TOKENS, SLOTS), BF16),
            vmem((TOKENS, SLOTS), F32),
            vmem((TOKENS, SLOTS), F32),
            vmem((TOKENS, SLOTS), F32),
            vmem((TOKENS, SLOTS), F32),
            vmem((TOKENS, D), F32),
            vmem((2, ROWS, HALF), BF16),
            vmem((2, ROWS, HALF), BF16),
            vmem((2, 8, 32, HALF), BF16),
            vmem((2, 2, ROWS, HALF), BF16),
            vmem((2, 2, ROWS, HALF), BF16),
            vmem((2, 2, ROWS, D), F32),
            vmem((2, ROWS, D), BF16),
            vmem((2, ROWS, D), F32),
            vmem((ROWS, D), F32),
            vmem((ROWS, D), BF16),
            vmem((ROWS, D), BF16),
            vmem((SLOTS, D), F32),
            vmem((SLOTS, D), F32),
            vmem((SLOTS, D), F32),
            vmem((SLOTS, 768), F32),
            vmem((SLOTS, 768), F32),
            vmem((SLOTS, 768), F32),
            vmem((8, 768), F32),
            vmem((64, 384), F32),
            sems((6,)),
            sems((NF,)), sems((NF,)), sems((NF,)), sems((NF,)), sems((NF,)), sems((NF,)),
            sems((NB,)), sems((NB,)), sems((NB,)), sems((NB,)), sems((NB,)), sems((NB,)),
            sems((4,)), sems((4,)),
            sems,
        ],
        compiler_params=pltpu.CompilerParams(
            collective_id=0, has_side_effects=True, vmem_limit_bytes=56 * 2**20
        ),
        name="soft_moe_backward",
    )(activations[0], out_grad[0], slot_out[0], slot_proj, w_in[0], w_out[0])
    return d_acts[None], d_proj.T


def solution(mesh):
    placed = (
        P(("ep", "tp"), None, None),
        P(("ep", "tp"), None, None),
        P(("ep", "tp"), None, None),
        P(),
        P("ep", None, "tp"),
        P("ep", "tp", None),
    )
    return jax.shard_map(
        local,
        mesh=mesh,
        in_specs=placed,
        out_specs=(P(("ep", "tp"), None, None), P("tp", "ep")),
        check_vma=False,
    )
```

time: 486 us -> 96.5 us (0.20)
  waiting for transfers between devices: 355 us -> 0 us
  Pallas kernels: 0 us -> 92.7 us
  blocking collectives: 48.8 us -> 0 us
  matrix products: 31 us -> 0 us
  local copies, waits for them, and re-layouts: 27.5 us -> 3.04 us
  between operations: 13.9 us -> 0.65 us
  starting transfers between devices: 8.32 us -> 0 us
    psum x1 -> x0, waiting for transfers between devices: 243 us -> none  [local(): summed_proj = lax.psum(proj_term, ('ep', 'tp'))]
    pallas_call x0 -> x1, Pallas kernels: none -> 92.7 us  [local(): pl.pallas_call(kernel, out_shape=(jax.ShapeDtypeStruct((TOKENS, D), F32),...]
    reduce_scatter x1 -> x0, waiting for transfers between devices: 59.5 us -> none  [local(): lax.psum_scatter(contract_last(pre_grad, first_proj), 'tp', scatter_dimen...]
    all_to_all x2 -> x0, blocking collectives: 48.8 us -> none  [the longest x1 24.7 us: local(): lax.all_to_all(slot_in.reshape(grouped), 'ep', split_axis=1, concat_axis=...]
    all_gather x2 -> x0, waiting for transfers between devices: 34.2 us -> none  [the longest x1 31.3 us: local(): all_grad = lax.all_gather(recv_grad, 'tp', axis=0, tiled=True)]
    dot_general x10 -> x0, matrix products: 31 us -> none  [the longest x1 8.36 us: contract_last(): lax.dot_general(left, right, (((1,), (1,)), ((), ())), preferred_element_...]
    all_to_all x1 -> x0, waiting for transfers between devices: 19 us -> none  [send_back(): return lax.all_to_all(summed, 'ep', split_axis=1, concat_axis=1, tiled=True)]
    reshape x5 -> x0, local copies, waits for them, and re-layouts: 14.1 us -> none  [the longest x1 4.06 us: local(): hidden_grad = contract_last(all_grad.reshape(-1, model_width), second_proj)]
  transfers between devices with their start and end apart: 5 -> 0, of which waited for: 5 -> 0; matrix products, arithmetic and copies ran while one was open for 4% -> 0% of each run, Pallas kernels for 0% -> 0%
where the time goes in v2:
time: 96.5 us; the launch traced here: 96.4 us
  Pallas kernels  92.7 us (96%)
  local copies, waits for them, and re-layouts  3.04 us (3%)
    pallas_call x1, Pallas kernels, local(): pl.pallas_call(kernel, out_shape=(jax.ShapeDtypeStruct((TOKENS, D), F32),...  92.7 us
    unnamed x4, local copies, waits for them, and re-layouts  3.04 us

profile of v2, /device:TPU:1, one launch (start us, length us, event | category | flops | bytes accessed | tf_op | source)
XLA Modules:
  0.0 96.4 jit_solution(14900764266029329397)
XLA Ops:
  0.6 92.7 %soft_moe_backward.1 = (f32[256,1280]{1,0:T(8,128)}, f32[2,320]{1,0:T(2,128)}) custom-call(f32[256,1280]{1,0:T(8,128)} %bitcast.9, f32[256,1280]{1,0:T(8,128)} %bitcast.10, f32[128,1280]{1,0:T(8,128)} %bitcast.12, f32[1280,128]{1,0:T(8,128)} %sp_hbm.1, bf16[1280,1280]{1,0:T(8,128)(2,1)} %bitcast.7, bf16[1280,1280]{1,0:T(8,128)(2,1)} %bitcast.8), custom_call_target="tpu_custom_call" | custom-call | tf_op jit(solution)/shard_map/soft_moe_backward/pallas_call | solution.py:421
  93.4 0.0 copy-start
  93.4 2.5 %copy.10 = f32[1,256,1280]{2,1,0:T(8,128)} copy(f32[1,256,1280]{2,1,0:T(8,128)} %bitcast.11) | data formatting | bytes 2621440
  95.9 0.0 copy-done
  95.9 0.6 copy.11
Async XLA Ops:
  93.4 2.5 %copy-start = (f32[2,320]{1,0:T(2,128)S(1)}, f32[2,320]{1,0:T(2,128)}, u32[]{:S(2)}) copy-start(f32[2,320]{1,0:T(2,128)} %get-tuple-element.5) | copy-start | bytes 7684

commit v3 on v2

v3 whole, which is shorter than its diff:
```python
import functools

import jax
import jax.numpy as jnp
from jax import lax
from jax.experimental import pallas as pl
from jax.experimental.pallas import tpu as pltpu
from jax.sharding import PartitionSpec as P

MESH = pl.DeviceIdType.MESH
F32 = jnp.float32
BF16 = jnp.bfloat16
D = 1280
HALF = 640
TOKENS = 256
SLOTS = 128
ROWS = 256
PLANE = 16
RING = 8
WIDE = 256
FORWARD = (
    (0, 0, 256), (0, 256, 256), (0, 512, 128),
    (1, 0, 256), (1, 256, 256), (1, 512, 128),
)
BACK = ((0, 256), (256, 256), (512, 128))
NF, NB = len(FORWARD), len(BACK)


def gelu_slope(pre_act):
    normal_cdf = 0.5 * (1.0 + lax.erf(pre_act * 0.7071067811865476))
    density = jnp.exp(-0.5 * pre_act * pre_act) * 0.3989422804014327
    return normal_cdf + pre_act * density


def dot_nn(a, b):
    return jnp.dot(a, b, preferred_element_type=F32)


def dot_nt(a, b):
    return lax.dot_general(a, b, (((1,), (1,)), ((), ())), preferred_element_type=F32)


def split(a):
    high = a.astype(BF16)
    return high, (a - high.astype(F32)).astype(BF16)


def three(dot, a, b):
    return dot(a[0], b[0]) + (dot(a[0], b[1]) + dot(a[1], b[0]))


def iota2(shape, axis):
    return lax.broadcasted_iota(jnp.int32, shape, axis)


def one_hot(condition):
    return jnp.where(condition, 1.0, 0.0).astype(BF16)


def kernel(
    acts_hbm, og_hbm, so_hbm, sp_hbm, wi_hbm, wo_hbm,
    dacts_hbm, dproj_ref,
    acts, og, so, sp, wi, wo,
    acts_s, og_s, so_s, sp_s, disp_s, disp, comb, comb_term, disp_grad, logit_grad, dacts,
    slots, send, plane_in, ring_out, ring_in, first_out, first_in, first_send, first_plane,
    acc, pre_grad, part, part_in, back_out, back_in, back_send, sig,
    dp_out, dp_own, dp_in, dp_sum, dp_plane, dp_ring, dp_back,
    load_sem, fps, fpr, fzs, fzr, fcs, fcr, bcs, bcr, bzs, bzr, bps, bpr, dps, dpr, out_sem,
):
    ep, tp = lax.axis_index("ep"), lax.axis_index("tp")
    z_lo, pos = lax.div(ep, 16), lax.rem(ep, 16)
    x, y = lax.div(pos, 4), lax.rem(pos, 4)
    z_hi, core = lax.div(tp, 2), lax.rem(tp, 2)
    z = z_hi * 4 + z_lo
    other = {"ep": ep, "tp": z_hi * 2 + (1 - core)}

    def plane_peer(q):
        there = lax.rem(x + lax.div(q, 4), 4) * 4 + lax.rem(y + lax.rem(q, 4), 4)
        return there, {"ep": z_lo * 16 + there, "tp": tp}

    def ring_peer(q):
        there = lax.rem(z + q, RING)
        lo = lax.rem(there, 4)
        return there, lo, {"ep": lo * 16 + pos, "tp": lax.div(there, 4) * 2 + core}

    def remote(src, dst, send_sem, recv_sem, device):
        return pltpu.make_async_remote_copy(
            src_ref=src, dst_ref=dst, send_sem=send_sem, recv_sem=recv_sem,
            device_id=device, device_id_type=MESH,
        )

    def wait_bytes(ref, sem):
        pltpu.make_async_copy(ref, ref, sem).wait()

    loads = []
    pairs = ((sp_hbm, sp), (acts_hbm, acts), (og_hbm, og), (so_hbm, so), (wi_hbm, wi), (wo_hbm, wo))
    for k, (src, dst) in enumerate(pairs):
        loads.append(pltpu.make_async_copy(src, dst, load_sem.at[k]))
        loads[-1].start()
    load_sp, load_acts, load_og, load_so, load_wi, load_wo = loads

    barrier = pltpu.get_barrier_semaphore()

    def greet_plane(q, carry):
        pl.semaphore_signal(barrier, inc=1, device_id=plane_peer(q)[1], device_id_type=MESH)
        return carry

    def greet_ring(q, carry):
        pl.semaphore_signal(barrier, inc=1, device_id=ring_peer(q)[2], device_id_type=MESH)
        return carry

    lax.fori_loop(1, PLANE, greet_plane, 0)
    lax.fori_loop(1, RING, greet_ring, 0)
    pl.semaphore_signal(barrier, inc=1, device_id=other, device_id_type=MESH)

    n, r = iota2((SLOTS, SLOTS), 0), iota2((SLOTS, SLOTS), 1)
    to_order = one_hot(n == lax.rem(r, 4) * 32 + lax.rem(lax.div(r, 4), 16) * 2 + lax.div(r, 64))
    to_order_t = one_hot(r == lax.rem(n, 4) * 32 + lax.rem(lax.div(n, 4), 16) * 2 + lax.div(n, 64))
    o, i = iota2((ROWS, ROWS), 0), iota2((ROWS, ROWS), 1)
    spread = one_hot(
        i == lax.rem(lax.div(o, 4), 4) * 64 + lax.div(o, 16) * 4 + lax.rem(o, 4)
    )
    regroup = one_hot(
        i == lax.rem(o, 16) * 16 + lax.rem(lax.div(o, 16), 4) * 4 + lax.div(o, 64)
    )
    direct = one_hot(
        i == lax.rem(lax.div(o, 16), 4) * 64 + lax.rem(o, 16) * 4 + lax.div(o, 64)
    )
    to_plane = one_hot(
        i == lax.rem(lax.div(o, 8), 2) * 128 + lax.rem(o, 8) * 16 + lax.div(o, 16)
    )
    from_plane = one_hot(
        o == lax.rem(lax.div(i, 8), 2) * 128 + lax.rem(i, 8) * 16 + lax.div(i, 16)
    )
    o, i = iota2((SLOTS, ROWS), 0), iota2((SLOTS, ROWS), 1)
    collect = one_hot(
        (lax.div(i, 128) == lax.rem(lax.div(o, 4), 2))
        & (lax.rem(i, 64) == lax.rem(o, 4) * 16 + lax.div(o, 8))
    )
    def place(s, h):
        return one_hot(
            (lax.div(n, 64) == s)
            & (r == lax.div(lax.rem(n, 64), 4) * 8 + h * 4 + lax.rem(n, 4))
        )

    def twice(s):
        return one_hot(r == s * 64 + lax.div(n, 8) * 4 + lax.rem(n, 4))

    load_sp.wait()
    for k, part_of in enumerate(split(sp[...])):
        sp_s[k] = dot_nn(part_of, to_order).astype(BF16)
    load_acts.wait()
    acts_s[0], acts_s[1] = split(acts[...])
    logits = three(dot_nn, (acts_s[0], acts_s[1]), (sp_s[0], sp_s[1]))
    e = jnp.exp(logits - jnp.max(logits, axis=0, keepdims=True))
    dispatch = e / jnp.sum(e, axis=0, keepdims=True)
    disp[...] = dispatch
    disp_s[0], disp_s[1] = split(dispatch)
    dispatch_t = split(dispatch.T)
    e = jnp.exp(logits - jnp.max(logits, axis=1, keepdims=True))
    combine = e / jnp.sum(e, axis=1, keepdims=True)
    comb[...] = combine
    combine_t = split(combine.T)
    load_og.wait()
    og_s[0], og_s[1] = split(og[...])

    def slot_rows(col, width):
        for kind, weights_t, values in ((0, dispatch_t, acts_s), (1, combine_t, og_s)):
            for h in range(2):
                c = h * HALF + col
                rows = three(
                    dot_nn, weights_t, (values[0, :, c : c + width], values[1, :, c : c + width])
                )
                slots[kind, :, c : c + width] = rows.astype(BF16)

    def across(k):
        s, col, width = FORWARD[k]
        return remote(
            ring_in.at[s, :, pl.ds(0, 128), pl.ds(col, width)],
            ring_in.at[s, :, pl.ds(128, 128), pl.ds(col, width)],
            fcs.at[k], fcr.at[k], other,
        )

    def stacked(k):
        s, col, width = FORWARD[k]
        parts = [
            slots[kind, s * 64 : s * 64 + 64, h * HALF + col : h * HALF + col + width]
            for h in range(2) for kind in range(2)
        ]
        return jnp.concatenate(parts, axis=0)

    def first_ring():
        rows = dot_nn(direct, stacked(0)).astype(BF16)
        first_out[...] = rows.reshape(16, 16, WIDE)
        pl.semaphore_wait(barrier, PLANE - 1 + RING - 1 + 1)

        def one(q, carry):
            there, lo, device = ring_peer(q)
            remote(
                first_out.at[pl.ds(lo * 4, 4)],
                first_in.at[:, pl.ds(z * 16, 16)],
                fzs.at[0], fzr.at[0], device,
            ).start()
            return carry

        lax.fori_loop(1, RING, one, 0)
        first_in[:, pl.ds(z * 16, 16)] = first_out[pl.ds(z_lo * 4, 4)]

    def first_spread():
        wait_bytes(first_in.at[:, pl.ds(0, 112)], fzr.at[0])
        for h in range(2):
            rows = first_in[2 * h : 2 * h + 2].reshape(ROWS, WIDE)
            first_send[h] = dot_nn(to_plane, rows).astype(BF16)

        def one(q, carry):
            there, device = plane_peer(q)
            remote(
                first_send.at[:, pl.ds(there * 16, 16)],
                first_plane.at[:, pl.ds(pos * 16, 16)],
                fps.at[0], fpr.at[0], device,
            ).start()
            return carry

        lax.fori_loop(1, PLANE, one, 0)
        first_plane[:, pl.ds(pos * 16, 16)] = first_send[:, pl.ds(pos * 16, 16)]

    def first_arrived():
        wait_bytes(first_plane.at[:, pl.ds(0, 240)], fpr.at[0])
        for h in range(2):
            rows = dot_nn(from_plane, first_plane[h]).astype(BF16)
            ring_in[0, 2 * h : 2 * h + 2, 0:128, 0:WIDE] = rows.reshape(2, 128, WIDE)
        across(0).start()

    def plane_send(k):
        s, col, width = FORWARD[k]
        send[s, :, col : col + width] = dot_nn(spread, stacked(k)).astype(BF16)

        def one(q, carry):
            there, device = plane_peer(q)
            remote(
                send.at[s, pl.ds(there * 16, 16), pl.ds(col, width)],
                plane_in.at[s, pl.ds(pos * 16, 16), pl.ds(col, width)],
                fps.at[k], fpr.at[k], device,
            ).start()
            return carry

        lax.fori_loop(1, PLANE, one, 0)
        plane_in[s, pl.ds(pos * 16, 16), pl.ds(col, width)] = send[
            s, pl.ds(pos * 16, 16), pl.ds(col, width)
        ]

    slot_rows(FORWARD[0][1], FORWARD[0][2])
    first_ring()
    for k in range(1, NF // 2):
        slot_rows(FORWARD[k][1], FORWARD[k][2])
        plane_send(k)
    for k in range(NF // 2, NF):
        plane_send(k)

    def ring_send(k):
        s, col, width = FORWARD[k]
        wait_bytes(plane_in.at[s, pl.ds(0, 240), pl.ds(col, width)], fpr.at[k])
        moved = dot_nn(regroup, plane_in[s, :, col : col + width])
        ring_out[s, :, :, col : col + width] = moved.astype(BF16).reshape(16, 16, width)

        def one(q, carry):
            there, lo, device = ring_peer(q)
            remote(
                ring_out.at[s, pl.ds(lo * 4, 4), :, pl.ds(col, width)],
                ring_in.at[s, :, pl.ds(z * 16, 16), pl.ds(col, width)],
                fzs.at[k], fzr.at[k], device,
            ).start()
            return carry

        lax.fori_loop(1, RING, one, 0)
        ring_in[s, :, pl.ds(z * 16, 16), pl.ds(col, width)] = ring_out[
            s, pl.ds(z_lo * 4, 4), :, pl.ds(col, width)
        ]

    ring_send(1)
    ring_send(2)
    first_spread()
    for k in range(NF // 2, NF):
        ring_send(k)

    load_so.wait()
    for k, part_of in enumerate(split(so[...])):
        so_s[k] = dot_nn(to_order_t, part_of).astype(BF16)
    comb_grad = three(dot_nt, (og_s[0], og_s[1]), (so_s[0], so_s[1]))
    combine = comb[...]
    comb_term[...] = combine * (
        comb_grad - jnp.sum(comb_grad * combine, axis=1, keepdims=True)
    )

    load_wi.wait()
    load_wo.wait()

    def ring_arrived(k):
        s, col, width = FORWARD[k]
        wait_bytes(ring_in.at[s, :, pl.ds(0, 112), pl.ds(col, width)], fzr.at[k])
        across(k).start()

    def expert(k):
        s, col, width = FORWARD[k]
        across(k).wait_recv()

        def tile(t, carry):
            c = pl.multiple_of(t * 256, 256)
            first, second = None, None
            for h in range(2):
                d = h * HALF + col
                rows_in = ring_in[s, 2 * h, :, col : col + width]
                rows_grad = ring_in[s, 2 * h + 1, :, col : col + width]
                one = dot_nn(rows_in, wi[pl.ds(d, width), pl.ds(c, 256)])
                two = dot_nt(rows_grad, wo[pl.ds(c, 256), pl.ds(d, width)])
                first = one if first is None else first + one
                second = two if second is None else second + two
            if col > 0:
                first = first + acc[0, s, :, pl.ds(c, 256)]
                second = second + acc[1, s, :, pl.ds(c, 256)]
            if col + width == HALF:
                pre_grad[s, :, pl.ds(c, 256)] = (second * gelu_slope(first)).astype(BF16)
            else:
                acc[0, s, :, pl.ds(c, 256)] = first
                acc[1, s, :, pl.ds(c, 256)] = second
            return carry

        lax.fori_loop(0, 5, tile, 0)

    def back_across(s, b):
        col, width = BACK[b]
        return remote(
            part.at[s, :, pl.ds(128, 128), pl.ds(col, width)],
            part_in.at[s, :, :, pl.ds(col, width)],
            bcs.at[s, b], bcr.at[s, b], other,
        )

    def expert_back(s, b):
        col, width = BACK[b]
        for h in range(2):
            part[s, h, :, col : col + width] = dot_nt(
                pre_grad[s], wi[h * HALF + col : h * HALF + col + width, :]
            )
        back_across(s, b).start()

    def back_ring(s, b):
        col, width = BACK[b]
        back_across(s, b).wait_recv()
        both = part[s, :, 0:128, col : col + width] + part_in[s, :, :, col : col + width]
        back_out[s, :, :, col : col + width] = both.astype(BF16)

        def one(q, carry):
            there, _, device = ring_peer(q)
            remote(
                back_out.at[s, :, pl.ds(there * 16, 16), pl.ds(col, width)],
                back_in.at[s, :, pl.ds(z * 16, 16), pl.ds(col, width)],
                bzs.at[s, b], bzr.at[s, b], device,
            ).start()
            return carry

        lax.fori_loop(1, RING, one, 0)
        back_in[s, :, pl.ds(z * 16, 16), pl.ds(col, width)] = back_out[
            s, :, pl.ds(z * 16, 16), pl.ds(col, width)
        ]

    def back_plane(s, b):
        col, width = BACK[b]
        wait_bytes(back_in.at[s, :, pl.ds(0, 112), pl.ds(col, width)], bzr.at[s, b])
        back_send[s, :, col : col + width] = dot_nn(
            collect, back_in[s, :, :, col : col + width].reshape(ROWS, width)
        )

        def one(q, carry):
            there, device = plane_peer(q)
            remote(
                back_send.at[s, pl.ds(there * 8, 8), pl.ds(col, width)],
                sig.at[s, pl.ds(pos * 8, 8), pl.ds(col, width)],
                bps.at[s, b], bpr.at[s, b], device,
            ).start()
            return carry

        lax.fori_loop(1, PLANE, one, 0)
        sig[s, pl.ds(pos * 8, 8), pl.ds(col, width)] = back_send[
            s, pl.ds(pos * 8, 8), pl.ds(col, width)
        ]

    def arrived(s, b):
        col, width = BACK[b]
        wait_bytes(sig.at[s, pl.ds(0, 120), pl.ds(col, width)], bpr.at[s, b])
        high, low = split(sig[s, :, col : col + width])
        for h in range(2):
            c = h * HALF + col
            there = place(s, h)
            grad = (dot_nn(there, high).astype(BF16), dot_nn(there, low).astype(BF16))
            tokens = (acts_s[0, :, c : c + width], acts_s[1, :, c : c + width])
            term = three(dot_nt, tokens, grad)
            if s == 0 and b == 0 and h == 0:
                disp_grad[...] = term
            else:
                disp_grad[...] += term
            term = three(dot_nn, (disp_s[0], disp_s[1]), grad)
            if s == 0:
                dacts[:, c : c + width] = term
            else:
                dacts[:, c : c + width] += term

    def proj_across(s):
        return remote(dp_out.at[s], dp_in.at[s], dps.at[s, 0], dpr.at[s, 0], other)

    def proj_start(s):
        dispatch = disp[...]
        grad = disp_grad[...]
        whole = comb_term[...] + dispatch * (
            grad - jnp.sum(grad * dispatch, axis=0, keepdims=True)
        )
        logit_grad[...] = whole
        rows = [dot_nn(twice(s), a).astype(BF16) for a in split(whole.T)]
        upper = lax.rem(lax.div(iota2((SLOTS, 384), 0), 4), 2) == 0

        def half(which):
            terms = []
            for k in range(2):
                cols = pl.ds(pl.multiple_of(k * HALF + which * 256, 128), 384)
                terms.append(three(dot_nn, rows, (acts_s[0, :, cols], acts_s[1, :, cols])))
            return jnp.where(upper, terms[0], terms[1])

        dp_out[s] = half(1 - core)
        proj_across(s).start()
        dp_own[s] = half(core)

    def proj_plane(s):
        proj_across(s).wait_recv()
        dp_sum[s] = dp_own[s] + dp_in[s]

        def one(q, carry):
            there, device = plane_peer(q)
            remote(
                dp_sum.at[s, pl.ds(there * 8, 8)], dp_plane.at[s, pl.ds(pos * 8, 8)],
                dps.at[s, 1], dpr.at[s, 1], device,
            ).start()
            return carry

        lax.fori_loop(1, PLANE, one, 0)
        dp_plane[s, pl.ds(pos * 8, 8)] = dp_sum[s, pl.ds(pos * 8, 8)]

    def proj_ring(s):
        wait_bytes(dp_plane.at[s, pl.ds(0, 120)], dpr.at[s, 1])
        dp_ring[s] = jnp.sum(dp_plane[s].reshape(PLANE, 8, 384), axis=0)

        def one(q, carry):
            there, _, device = ring_peer(q)
            remote(
                dp_ring.at[s], dp_back.at[s, pl.ds(z * 8, 8)],
                dps.at[s, 2], dpr.at[s, 2], device,
            ).start()
            return carry

        lax.fori_loop(1, RING, one, 0)
        dp_back[s, pl.ds(z * 8, 8)] = dp_ring[s]

    def proj_end(s):
        wait_bytes(dp_back.at[s, pl.ds(0, 56)], dpr.at[s, 2])
        total = jnp.sum(dp_back[s].reshape(RING, 8, 384), axis=0)
        mine = jnp.sum(
            jnp.where(iota2((8, 384), 0) == z, total, 0.0), axis=0, keepdims=True
        )
        dproj_ref[s : s + 1, :] = jnp.where(core == 0, mine[:, 0:320], mine[:, 64:384])

    first_arrived()
    expert(0)
    for k in range(1, NF // 2):
        ring_arrived(k)
        expert(k)
    for b in range(NB):
        expert_back(0, b)
    ring_arrived(3)
    expert(3)
    ring_arrived(4)
    for b in range(NB):
        back_ring(0, b)
    expert(4)
    ring_arrived(5)
    expert(5)
    for b in range(NB):
        expert_back(1, b)
        if b > 0:
            back_ring(1, b - 1)
    back_ring(1, NB - 1)
    for s in range(2):
        for b in range(NB):
            back_plane(s, b)
    for b in range(NB):
        arrived(0, b)
    proj_start(0)
    proj_plane(0)
    for b in range(NB):
        arrived(1, b)
    proj_start(1)
    proj_ring(0)
    proj_plane(1)
    whole = split(logit_grad[...])
    for c in range(0, D, 256):
        dacts[:, c : c + 256] += three(
            dot_nt, whole, (sp_s[0, c : c + 256, :], sp_s[1, c : c + 256, :])
        )
    store = pltpu.make_async_copy(dacts, dacts_hbm, out_sem)
    store.start()
    proj_ring(1)
    proj_end(0)
    proj_end(1)

    for k in range(NF):
        s, col, width = FORWARD[k]
        if k == 0:
            wait_bytes(first_plane.at[:, pl.ds(0, 240)], fps.at[k])
            wait_bytes(first_in.at[:, pl.ds(0, 112)], fzs.at[k])
        else:
            wait_bytes(plane_in.at[s, pl.ds(0, 240), pl.ds(col, width)], fps.at[k])
            wait_bytes(ring_in.at[s, :, pl.ds(0, 112), pl.ds(col, width)], fzs.at[k])
        across(k).wait_send()
    for s in range(2):
        for b in range(NB):
            col, width = BACK[b]
            back_across(s, b).wait_send()
            wait_bytes(back_in.at[s, :, pl.ds(0, 112), pl.ds(col, width)], bzs.at[s, b])
            wait_bytes(sig.at[s, pl.ds(0, 120), pl.ds(col, width)], bps.at[s, b])
        proj_across(s).wait_send()
        wait_bytes(dp_plane.at[s, pl.ds(0, 120)], dps.at[s, 1])
        wait_bytes(dp_back.at[s, pl.ds(0, 56)], dps.at[s, 2])
    store.wait()


def local(activations, out_grad, slot_out, slot_proj, w_in, w_out):
    vmem = pltpu.VMEM
    sems = pltpu.SemaphoreType.DMA
    any_space = pl.BlockSpec(memory_space=pl.ANY)
    d_acts, d_proj = pl.pallas_call(
        kernel,
        out_shape=(
            jax.ShapeDtypeStruct((TOKENS, D), F32),
            jax.ShapeDtypeStruct((2, 320), F32),
        ),
        in_specs=[any_space] * 6,
        out_specs=(any_space, pl.BlockSpec(memory_space=pltpu.VMEM)),
        scratch_shapes=[
            vmem((TOKENS, D), F32),
            vmem((TOKENS, D), F32),
            vmem((SLOTS, D), F32),
            vmem((D, SLOTS), F32),
            vmem((D, D), BF16),
            vmem((D, D), BF16),
            vmem((2, TOKENS, D), BF16),
            vmem((2, TOKENS, D), BF16),
            vmem((2, SLOTS, D), BF16),
            vmem((2, D, SLOTS), BF16),
            vmem((2, TOKENS, SLOTS), BF16),
            vmem((TOKENS, SLOTS), F32),
            vmem((TOKENS, SLOTS), F32),
            vmem((TOKENS, SLOTS), F32),
            vmem((TOKENS, SLOTS), F32),
            vmem((TOKENS, SLOTS), F32),
            vmem((TOKENS, D), F32),
            vmem((2, SLOTS, D), BF16),
            vmem((2, ROWS, HALF), BF16),
            vmem((2, ROWS, HALF), BF16),
            vmem((2, 16, 16, HALF), BF16),
            vmem((2, 4, ROWS, HALF), BF16),
            vmem((16, 16, WIDE), BF16),
            vmem((4, 128, WIDE), BF16),
            vmem((2, ROWS, WIDE), BF16),
            vmem((2, ROWS, WIDE), BF16),
            vmem((2, 2, ROWS, D), F32),
            vmem((2, ROWS, D), BF16),
            vmem((2, 2, ROWS, HALF), F32),
            vmem((2, 2, 128, HALF), F32),
            vmem((2, 2, 128, HALF), BF16),
            vmem((2, 2, 128, HALF), BF16),
            vmem((2, SLOTS, HALF), F32),
            vmem((2, SLOTS, HALF), F32),
            vmem((2, SLOTS, 384), F32),
            vmem((2, SLOTS, 384), F32),
            vmem((2, SLOTS, 384), F32),
            vmem((2, SLOTS, 384), F32),
            vmem((2, SLOTS, 384), F32),
            vmem((2, 8, 384), F32),
            vmem((2, 64, 384), F32),
            sems((6,)),
            sems((NF,)), sems((NF,)), sems((NF,)), sems((NF,)), sems((NF,)), sems((NF,)),
            sems((2, NB)), sems((2, NB)), sems((2, NB)), sems((2, NB)), sems((2, NB)), sems((2, NB)),
            sems((2, 3)), sems((2, 3)),
            sems,
        ],
        compiler_params=pltpu.CompilerParams(
            collective_id=0, has_side_effects=True, vmem_limit_bytes=56 * 2**20
        ),
        name="soft_moe_backward",
    )(activations[0], out_grad[0], slot_out[0], slot_proj, w_in[0], w_out[0])
    return d_acts[None], d_proj.T


def solution(mesh):
    placed = (
        P(("ep", "tp"), None, None),
        P(("ep", "tp"), None, None),
        P(("ep", "tp"), None, None),
        P(),
        P("ep", None, "tp"),
        P("ep", "tp", None),
    )
    return jax.shard_map(
        local,
        mesh=mesh,
        in_specs=placed,
        out_specs=(P(("ep", "tp"), None, None), P("tp", "ep")),
        check_vma=False,
    )
```

time: 96.5 us -> 84.5 us (0.88)
  Pallas kernels: 92.7 us -> 80.1 us
    pallas_call x1, Pallas kernels: 92.7 us -> 80.1 us  [local(): pl.pallas_call(kernel, out_shape=(jax.ShapeDtypeStruct((TOKENS, D), F32),...]
where the time goes in v3:
time: 84.5 us; the launch traced here: 83.8 us
  Pallas kernels  80.1 us (95%)
  local copies, waits for them, and re-layouts  3.04 us (4%)
    pallas_call x1, Pallas kernels, local(): pl.pallas_call(kernel, out_shape=(jax.ShapeDtypeStruct((TOKENS, D), F32),...  80.1 us
    unnamed x4, local copies, waits for them, and re-layouts  3.04 us

profile of v3, /device:TPU:1, one launch (start us, length us, event | category | flops | bytes accessed | tf_op | source)
XLA Modules:
  0.0 83.8 jit_solution(15930739130278687949)
XLA Ops:
  0.6 80.1 %soft_moe_backward.1 = (f32[256,1280]{1,0:T(8,128)}, f32[2,320]{1,0:T(2,128)}) custom-call(f32[256,1280]{1,0:T(8,128)} %bitcast.9, f32[256,1280]{1,0:T(8,128)} %bitcast.10, f32[128,1280]{1,0:T(8,128)} %bitcast.12, f32[1280,128]{1,0:T(8,128)} %sp_hbm.1, bf16[1280,1280]{1,0:T(8,128)(2,1)} %bitcast.7, bf16[1280,1280]{1,0:T(8,128)(2,1)} %bitcast.8), custom_call_target="tpu_custom_call" | custom-call | tf_op jit(solution)/shard_map/soft_moe_backward/pallas_call | solution.py:537
  80.7 0.0 copy-start
  80.8 2.5 %copy.10 = f32[1,256,1280]{2,1,0:T(8,128)} copy(f32[1,256,1280]{2,1,0:T(8,128)} %bitcast.11) | data formatting | bytes 2621440
  83.2 0.0 copy-done
  83.2 0.6 copy.11
Async XLA Ops:
  80.7 2.5 %copy-start = (f32[2,320]{1,0:T(2,128)S(1)}, f32[2,320]{1,0:T(2,128)}, u32[]{:S(2)}) copy-start(f32[2,320]{1,0:T(2,128)} %get-tuple-element.5) | copy-start | bytes 7684

commit v4 on v3

--- a/solution.py
+++ b/solution.py
@@ -59,13 +59,13 @@
 
 def kernel(
     acts_hbm, og_hbm, so_hbm, sp_hbm, wi_hbm, wo_hbm,
-    dacts_hbm, dproj_ref,
+    dacts, dproj_ref,
     acts, og, so, sp, wi, wo,
-    acts_s, og_s, so_s, sp_s, disp_s, disp, comb, comb_term, disp_grad, logit_grad, dacts,
+    acts_s, og_s, so_s, sp_s, disp_s, disp, comb, comb_term, disp_grad, logit_grad, grad_s,
     slots, send, plane_in, ring_out, ring_in, first_out, first_in, first_send, first_plane,
     acc, pre_grad, part, part_in, back_out, back_in, back_send, sig,
     dp_out, dp_own, dp_in, dp_sum, dp_plane, dp_ring, dp_back,
-    load_sem, fps, fpr, fzs, fzr, fcs, fcr, bcs, bcr, bzs, bzr, bps, bpr, dps, dpr, out_sem,
+    load_sem, fps, fpr, fzs, fzr, fcs, fcr, bcs, bcr, bzs, bzr, bps, bpr, dps, dpr,
 ):
     ep, tp = lax.axis_index("ep"), lax.axis_index("tp")
     z_lo, pos = lax.div(ep, 16), lax.rem(ep, 16)
@@ -162,9 +162,11 @@
     comb[...] = combine
     combine_t = split(combine.T)
     load_og.wait()
-    og_s[0], og_s[1] = split(og[...])
 
     def slot_rows(col, width):
+        for h in range(2):
+            c = h * HALF + col
+            og_s[0, :, c : c + width], og_s[1, :, c : c + width] = split(og[:, c : c + width])
         for kind, weights_t, values in ((0, dispatch_t, acts_s), (1, combine_t, og_s)):
             for h in range(2):
                 c = h * HALF + col
@@ -398,11 +400,8 @@
                 disp_grad[...] = term
             else:
                 disp_grad[...] += term
-            term = three(dot_nn, (disp_s[0], disp_s[1]), grad)
-            if s == 0:
-                dacts[:, c : c + width] = term
-            else:
-                dacts[:, c : c + width] += term
+            for k in range(2):
+                grad_s[k, s * 64 : s * 64 + 64, c : c + width] = grad[k][s * 64 : s * 64 + 64]
 
     def proj_across(s):
         return remote(dp_out.at[s], dp_in.at[s], dps.at[s, 0], dpr.at[s, 0], other)
@@ -467,44 +466,44 @@
         dproj_ref[s : s + 1, :] = jnp.where(core == 0, mine[:, 0:320], mine[:, 64:384])
 
     first_arrived()
-    expert(0)
-    for k in range(1, NF // 2):
+    for k in range(1, NF // 2 + 1):
         ring_arrived(k)
-        expert(k)
+        expert(k - 1)
     for b in range(NB):
         expert_back(0, b)
-    ring_arrived(3)
-    expert(3)
     ring_arrived(4)
     for b in range(NB):
         back_ring(0, b)
+    expert(3)
+    ring_arrived(5)
     expert(4)
-    ring_arrived(5)
     expert(5)
     for b in range(NB):
         expert_back(1, b)
         if b > 0:
             back_ring(1, b - 1)
     back_ring(1, NB - 1)
-    for s in range(2):
-        for b in range(NB):
-            back_plane(s, b)
     for b in range(NB):
-        arrived(0, b)
+        back_plane(0, b)
+    back_plane(1, 0)
+    arrived(0, 0)
+    arrived(0, 1)
+    back_plane(1, 1)
+    arrived(0, 2)
+    back_plane(1, 2)
     proj_start(0)
+    arrived(1, 0)
     proj_plane(0)
-    for b in range(NB):
-        arrived(1, b)
+    arrived(1, 1)
+    arrived(1, 2)
     proj_start(1)
+    proj_plane(1)
     proj_ring(0)
-    proj_plane(1)
     whole = split(logit_grad[...])
     for c in range(0, D, 256):
-        dacts[:, c : c + 256] += three(
-            dot_nt, whole, (sp_s[0, c : c + 256, :], sp_s[1, c : c + 256, :])
-        )
-    store = pltpu.make_async_copy(dacts, dacts_hbm, out_sem)
-    store.start()
+        dacts[:, c : c + 256] = three(
+            dot_nn, (disp_s[0], disp_s[1]), (grad_s[0, :, c : c + 256], grad_s[1, :, c : c + 256])
+        ) + three(dot_nt, whole, (sp_s[0, c : c + 256, :], sp_s[1, c : c + 256, :]))
     proj_ring(1)
     proj_end(0)
     proj_end(1)
@@ -527,7 +526,6 @@
         proj_across(s).wait_send()
         wait_bytes(dp_plane.at[s, pl.ds(0, 120)], dps.at[s, 1])
         wait_bytes(dp_back.at[s, pl.ds(0, 56)], dps.at[s, 2])
-    store.wait()
 
 
 def local(activations, out_grad, slot_out, slot_proj, w_in, w_out):
@@ -537,11 +535,11 @@
     d_acts, d_proj = pl.pallas_call(
         kernel,
         out_shape=(
-            jax.ShapeDtypeStruct((TOKENS, D), F32),
-            jax.ShapeDtypeStruct((2, 320), F32),
+            pltpu.VMEM((TOKENS, D), F32),
+            pltpu.VMEM((2, 320), F32),
         ),
         in_specs=[any_space] * 6,
-        out_specs=(any_space, pl.BlockSpec(memory_space=pltpu.VMEM)),
+        out_specs=(pl.BlockSpec(memory_space=pltpu.VMEM),) * 2,
         scratch_shapes=[
             vmem((TOKENS, D), F32),
             vmem((TOKENS, D), F32),
@@ -559,7 +557,7 @@
             vmem((TOKENS, SLOTS), F32),
             vmem((TOKENS, SLOTS), F32),
             vmem((TOKENS, SLOTS), F32),
-            vmem((TOKENS, D), F32),
+            vmem((2, SLOTS, D), BF16),
             vmem((2, SLOTS, D), BF16),
             vmem((2, ROWS, HALF), BF16),
             vmem((2, ROWS, HALF), BF16),
@@ -588,7 +586,6 @@
             sems((NF,)), sems((NF,)), sems((NF,)), sems((NF,)), sems((NF,)), sems((NF,)),
             sems((2, NB)), sems((2, NB)), sems((2, NB)), sems((2, NB)), sems((2, NB)), sems((2, NB)),
             sems((2, 3)), sems((2, 3)),
-            sems,
         ],
         compiler_params=pltpu.CompilerParams(
             collective_id=0, has_side_effects=True, vmem_limit_bytes=56 * 2**20

time: 84.5 us -> 80.6 us (0.954)
  Pallas kernels: 80.1 us -> 78.2 us
  local copies, waits for them, and re-layouts: 3.04 us -> 1.64 us
    pallas_call x1, Pallas kernels: 80.1 us -> 78.2 us  [local(): pl.pallas_call(kernel, out_shape=(pltpu.VMEM((TOKENS, D), F32), pltpu.VME...]
    unnamed x4 -> x2, local copies, waits for them, and re-layouts: 3.04 us -> 1.64 us
where the time goes in v4:
time: 80.6 us; the launch traced here: 80.5 us
  Pallas kernels  78.2 us (97%)
  local copies, waits for them, and re-layouts  1.64 us (2%)
    pallas_call x1, Pallas kernels, local(): pl.pallas_call(kernel, out_shape=(pltpu.VMEM((TOKENS, D), F32), pltpu.VME...  78.2 us
    unnamed x2, local copies, waits for them, and re-layouts  1.64 us

profile of v4, /device:TPU:1, one launch (start us, length us, event | category | flops | bytes accessed | tf_op | source)
XLA Modules:
  0.0 80.5 jit_solution(6486044341170981237)
XLA Ops:
  0.6 78.2 %soft_moe_backward.1 = (f32[256,1280]{1,0:T(8,128)S(1)}, f32[2,320]{1,0:T(2,128)S(1)}) custom-call(f32[256,1280]{1,0:T(8,128)} %bitcast.11, f32[256,1280]{1,0:T(8,128)} %bitcast.12, f32[128,1280]{1,0:T(8,128)} %bitcast.13, f32[1280,128]{1,0:T(8,128)} %sp_hbm.1, bf16[1280,1280]{1,0:T(8,128)(2,1)} %bitcast.9, bf16[1280,1280]{1,0:T(8,128)(2,1)} %bitcast.10), custom_call_target="tpu_custom_call" | custom-call | tf_op jit(solution)/shard_map/soft_moe_backward/pallas_call | solution.py:535
  78.9 1.1 %copy.10 = f32[1,256,1280]{2,1,0:T(8,128)} copy(f32[1,256,1280]{2,1,0:T(8,128)S(1)} %bitcast.7) | data formatting | bytes 2621440
  79.9 0.6 copy.11

commit v5 on v4

--- a/solution.py
+++ b/solution.py
@@ -18,11 +18,17 @@
 PLANE = 16
 RING = 8
 WIDE = 256
+BLOCKS_A = ((0, 0), (0, 256), (0, 512), (0, 768))
+BLOCKS_A1 = ((0, 0), (0, 128), (0, 256), (0, 384))
+BLOCKS_A2 = ((0, 512), (0, 640), (0, 768), (0, 896))
+BLOCKS_B = ((0, 1024), (1, 0), (1, 256), (1, 512))
+BLOCKS_C = ((1, 768), (1, 896), (1, 1024), (1, 1152))
 FORWARD = (
-    (0, 0, 256), (0, 256, 256), (0, 512, 128),
-    (1, 0, 256), (1, 256, 256), (1, 512, 128),
+    (0, 0, 256, BLOCKS_A), (1, 0, 128, BLOCKS_A1),
+    (0, 256, 256, BLOCKS_B), (0, 512, 128, BLOCKS_C),
+    (1, 128, 128, BLOCKS_A2), (1, 256, 256, BLOCKS_B), (1, 512, 128, BLOCKS_C),
 )
-BACK = ((0, 256), (256, 256), (512, 128))
+BACK = ((0, 128), (128, 256), (384, 128), (512, 128))
 NF, NB = len(FORWARD), len(BACK)
 
 
@@ -64,7 +70,7 @@
     acts_s, og_s, so_s, sp_s, disp_s, disp, comb, comb_term, disp_grad, logit_grad, grad_s,
     slots, send, plane_in, ring_out, ring_in, first_out, first_in, first_send, first_plane,
     acc, pre_grad, part, part_in, back_out, back_in, back_send, sig,
-    dp_out, dp_own, dp_in, dp_sum, dp_plane, dp_ring, dp_back,
+    dp_out, dp_own, dp_in, dp_sum, dp_plane, dp_pack, dp_back,
     load_sem, fps, fpr, fzs, fzr, fcs, fcr, bcs, bcr, bzs, bzr, bps, bpr, dps, dpr,
 ):
     ep, tp = lax.axis_index("ep"), lax.axis_index("tp")
@@ -74,11 +80,13 @@
     z = z_hi * 4 + z_lo
     other = {"ep": ep, "tp": z_hi * 2 + (1 - core)}
 
-    def plane_peer(q):
+    def plane_peer(i):
+        q = 1 + lax.rem(i + 8, PLANE - 1)
         there = lax.rem(x + lax.div(q, 4), 4) * 4 + lax.rem(y + lax.rem(q, 4), 4)
         return there, {"ep": z_lo * 16 + there, "tp": tp}
 
-    def ring_peer(q):
+    def ring_peer(i):
+        q = 1 + lax.rem(i + 2, RING - 1)
         there = lax.rem(z + q, RING)
         lo = lax.rem(there, 4)
         return there, lo, {"ep": lo * 16 + pos, "tp": lax.div(there, 4) * 2 + core}
@@ -96,7 +104,8 @@
     pairs = ((sp_hbm, sp), (acts_hbm, acts), (og_hbm, og), (so_hbm, so), (wi_hbm, wi), (wo_hbm, wo))
     for k, (src, dst) in enumerate(pairs):
         loads.append(pltpu.make_async_copy(src, dst, load_sem.at[k]))
-        loads[-1].start()
+        if k < 3:
+            loads[-1].start()
     load_sp, load_acts, load_og, load_so, load_wi, load_wo = loads
 
     barrier = pltpu.get_barrier_semaphore()
@@ -109,8 +118,8 @@
         pl.semaphore_signal(barrier, inc=1, device_id=ring_peer(q)[2], device_id_type=MESH)
         return carry
 
-    lax.fori_loop(1, PLANE, greet_plane, 0)
-    lax.fori_loop(1, RING, greet_ring, 0)
+    lax.fori_loop(0, PLANE - 1, greet_plane, 0)
+    lax.fori_loop(0, RING - 1, greet_ring, 0)
     pl.semaphore_signal(barrier, inc=1, device_id=other, device_id_type=MESH)
 
     n, r = iota2((SLOTS, SLOTS), 0), iota2((SLOTS, SLOTS), 1)
@@ -146,10 +155,13 @@
     def twice(s):
         return one_hot(r == s * 64 + lax.div(n, 8) * 4 + lax.rem(n, 4))
 
+    dp_pack[...] = jnp.zeros_like(dp_pack)
     load_sp.wait()
     for k, part_of in enumerate(split(sp[...])):
         sp_s[k] = dot_nn(part_of, to_order).astype(BF16)
     load_acts.wait()
+    for late in (load_so, load_wi, load_wo):
+        late.start()
     acts_s[0], acts_s[1] = split(acts[...])
     logits = three(dot_nn, (acts_s[0], acts_s[1]), (sp_s[0], sp_s[1]))
     e = jnp.exp(logits - jnp.max(logits, axis=0, keepdims=True))
@@ -157,110 +169,112 @@
     disp[...] = dispatch
     disp_s[0], disp_s[1] = split(dispatch)
     dispatch_t = split(dispatch.T)
+
+    def slot_rows(kind, weights_t, values, c):
+        rows = three(dot_nn, weights_t, (values[0, :, c : c + WIDE], values[1, :, c : c + WIDE]))
+        slots[kind, :, c : c + WIDE] = rows.astype(BF16)
+
+    def across(k):
+        s, col, width, blocks = FORWARD[k]
+        return remote(
+            ring_in.at[s, :, pl.ds(0, 128), pl.ds(col, width)],
+            ring_in.at[s, :, pl.ds(128, 128), pl.ds(col, width)],
+            fcs.at[k], fcr.at[k], other,
+        )
+
+    def stacked(k):
+        s, col, width, blocks = FORWARD[k]
+        parts = [
+            slots[kind, s * 64 : s * 64 + 64, c : c + width] for kind, c in blocks
+        ]
+        return jnp.concatenate(parts, axis=0)
+
+    def first_ring(k):
+        width = FORWARD[k][2]
+        rows = dot_nn(direct, stacked(k)).astype(BF16)
+        first_out[k, :, :, 0:width] = rows.reshape(16, 16, width)
+        if k == 0:
+            pl.semaphore_wait(barrier, PLANE - 1 + RING - 1 + 1)
+
+        def one(q, carry):
+            there, lo, device = ring_peer(q)
+            remote(
+                first_out.at[k, pl.ds(lo * 4, 4), :, pl.ds(0, width)],
+                first_in.at[k, :, pl.ds(z * 16, 16), pl.ds(0, width)],
+                fzs.at[k], fzr.at[k], device,
+            ).start()
+            return carry
+
+        lax.fori_loop(0, RING - 1, one, 0)
+        first_in[k, :, pl.ds(z * 16, 16), 0:width] = first_out[k, pl.ds(z_lo * 4, 4), :, 0:width]
+
+    def first_spread(k):
+        width = FORWARD[k][2]
+        wait_bytes(first_in.at[k, :, pl.ds(0, 112), pl.ds(0, width)], fzr.at[k])
+        for h in range(2):
+            rows = first_in[k, 2 * h : 2 * h + 2, :, 0:width].reshape(ROWS, width)
+            first_send[k, h, :, 0:width] = dot_nn(to_plane, rows).astype(BF16)
+
+        def one(q, carry):
+            there, device = plane_peer(q)
+            remote(
+                first_send.at[k, :, pl.ds(there * 16, 16), pl.ds(0, width)],
+                first_plane.at[k, :, pl.ds(pos * 16, 16), pl.ds(0, width)],
+                fps.at[k], fpr.at[k], device,
+            ).start()
+            return carry
+
+        lax.fori_loop(0, PLANE - 1, one, 0)
+        first_plane[k, :, pl.ds(pos * 16, 16), 0:width] = first_send[
+            k, :, pl.ds(pos * 16, 16), 0:width
+        ]
+
+    def first_arrived(k):
+        s, col, width, blocks = FORWARD[k]
+        wait_bytes(first_plane.at[k, :, pl.ds(0, 240), pl.ds(0, width)], fpr.at[k])
+        for h in range(2):
+            rows = dot_nn(from_plane, first_plane[k, h, :, 0:width]).astype(BF16)
+            ring_in[s, 2 * h : 2 * h + 2, 0:128, col : col + width] = rows.reshape(2, 128, width)
+        across(k).start()
+
+    def plane_send(k):
+        s, col, width, blocks = FORWARD[k]
+        send[s, :, col : col + width] = dot_nn(spread, stacked(k)).astype(BF16)
+
+        def one(q, carry):
+            there, device = plane_peer(q)
+            remote(
+                send.at[s, pl.ds(there * 16, 16), pl.ds(col, width)],
+                plane_in.at[s, pl.ds(pos * 16, 16), pl.ds(col, width)],
+                fps.at[k], fpr.at[k], device,
+            ).start()
+            return carry
+
+        lax.fori_loop(0, PLANE - 1, one, 0)
+        plane_in[s, pl.ds(pos * 16, 16), pl.ds(col, width)] = send[
+            s, pl.ds(pos * 16, 16), pl.ds(col, width)
+        ]
+
+    for c in range(0, D - WIDE, WIDE):
+        slot_rows(0, dispatch_t, acts_s, c)
+    first_ring(0)
+    first_ring(1)
+    slot_rows(0, dispatch_t, acts_s, D - WIDE)
     e = jnp.exp(logits - jnp.max(logits, axis=1, keepdims=True))
     combine = e / jnp.sum(e, axis=1, keepdims=True)
     comb[...] = combine
     combine_t = split(combine.T)
     load_og.wait()
-
-    def slot_rows(col, width):
-        for h in range(2):
-            c = h * HALF + col
-            og_s[0, :, c : c + width], og_s[1, :, c : c + width] = split(og[:, c : c + width])
-        for kind, weights_t, values in ((0, dispatch_t, acts_s), (1, combine_t, og_s)):
-            for h in range(2):
-                c = h * HALF + col
-                rows = three(
-                    dot_nn, weights_t, (values[0, :, c : c + width], values[1, :, c : c + width])
-                )
-                slots[kind, :, c : c + width] = rows.astype(BF16)
-
-    def across(k):
-        s, col, width = FORWARD[k]
-        return remote(
-            ring_in.at[s, :, pl.ds(0, 128), pl.ds(col, width)],
-            ring_in.at[s, :, pl.ds(128, 128), pl.ds(col, width)],
-            fcs.at[k], fcr.at[k], other,
-        )
-
-    def stacked(k):
-        s, col, width = FORWARD[k]
-        parts = [
-            slots[kind, s * 64 : s * 64 + 64, h * HALF + col : h * HALF + col + width]
-            for h in range(2) for kind in range(2)
-        ]
-        return jnp.concatenate(parts, axis=0)
-
-    def first_ring():
-        rows = dot_nn(direct, stacked(0)).astype(BF16)
-        first_out[...] = rows.reshape(16, 16, WIDE)
-        pl.semaphore_wait(barrier, PLANE - 1 + RING - 1 + 1)
-
-        def one(q, carry):
-            there, lo, device = ring_peer(q)
-            remote(
-                first_out.at[pl.ds(lo * 4, 4)],
-                first_in.at[:, pl.ds(z * 16, 16)],
-                fzs.at[0], fzr.at[0], device,
-            ).start()
-            return carry
-
-        lax.fori_loop(1, RING, one, 0)
-        first_in[:, pl.ds(z * 16, 16)] = first_out[pl.ds(z_lo * 4, 4)]
-
-    def first_spread():
-        wait_bytes(first_in.at[:, pl.ds(0, 112)], fzr.at[0])
-        for h in range(2):
-            rows = first_in[2 * h : 2 * h + 2].reshape(ROWS, WIDE)
-            first_send[h] = dot_nn(to_plane, rows).astype(BF16)
-
-        def one(q, carry):
-            there, device = plane_peer(q)
-            remote(
-                first_send.at[:, pl.ds(there * 16, 16)],
-                first_plane.at[:, pl.ds(pos * 16, 16)],
-                fps.at[0], fpr.at[0], device,
-            ).start()
-            return carry
-
-        lax.fori_loop(1, PLANE, one, 0)
-        first_plane[:, pl.ds(pos * 16, 16)] = first_send[:, pl.ds(pos * 16, 16)]
-
-    def first_arrived():
-        wait_bytes(first_plane.at[:, pl.ds(0, 240)], fpr.at[0])
-        for h in range(2):
-            rows = dot_nn(from_plane, first_plane[h]).astype(BF16)
-            ring_in[0, 2 * h : 2 * h + 2, 0:128, 0:WIDE] = rows.reshape(2, 128, WIDE)
-        across(0).start()
-
-    def plane_send(k):
-        s, col, width = FORWARD[k]
-        send[s, :, col : col + width] = dot_nn(spread, stacked(k)).astype(BF16)
-
-        def one(q, carry):
-            there, device = plane_peer(q)
-            remote(
-                send.at[s, pl.ds(there * 16, 16), pl.ds(col, width)],
-                plane_in.at[s, pl.ds(pos * 16, 16), pl.ds(col, width)],
-                fps.at[k], fpr.at[k], device,
-            ).start()
-            return carry
-
-        lax.fori_loop(1, PLANE, one, 0)
-        plane_in[s, pl.ds(pos * 16, 16), pl.ds(col, width)] = send[
-            s, pl.ds(pos * 16, 16), pl.ds(col, width)
-        ]
-
-    slot_rows(FORWARD[0][1], FORWARD[0][2])
-    first_ring()
-    for k in range(1, NF // 2):
-        slot_rows(FORWARD[k][1], FORWARD[k][2])
+    for c in range(0, D, WIDE):
+        og_s[0, :, c : c + WIDE], og_s[1, :, c : c + WIDE] = split(og[:, c : c + WIDE])
+        slot_rows(1, combine_t, og_s, c)
+        if c == 512:
+            plane_send(2)
+    for k in range(3, NF):
         plane_send(k)
-    for k in range(NF // 2, NF):
-        plane_send(k)
 
     def ring_send(k):
-        s, col, width = FORWARD[k]
+        s, col, width, blocks = FORWARD[k]
         wait_bytes(plane_in.at[s, pl.ds(0, 240), pl.ds(col, width)], fpr.at[k])
         moved = dot_nn(regroup, plane_in[s, :, col : col + width])
         ring_out[s, :, :, col : col + width] = moved.astype(BF16).reshape(16, 16, width)
@@ -274,15 +288,14 @@
             ).start()
             return carry
 
-        lax.fori_loop(1, RING, one, 0)
+        lax.fori_loop(0, RING - 1, one, 0)
         ring_in[s, :, pl.ds(z * 16, 16), pl.ds(col, width)] = ring_out[
             s, pl.ds(z_lo * 4, 4), :, pl.ds(col, width)
         ]
 
-    ring_send(1)
     ring_send(2)
-    first_spread()
-    for k in range(NF // 2, NF):
+    first_spread(0)
+    for k in range(3, NF):
         ring_send(k)
 
     load_so.wait()
@@ -298,33 +311,38 @@
     load_wo.wait()
 
     def ring_arrived(k):
-        s, col, width = FORWARD[k]
+        s, col, width, blocks = FORWARD[k]
         wait_bytes(ring_in.at[s, :, pl.ds(0, 112), pl.ds(col, width)], fzr.at[k])
         across(k).start()
 
     def expert(k):
-        s, col, width = FORWARD[k]
+        s, col, width, blocks = FORWARD[k]
         across(k).wait_recv()
 
         def tile(t, carry):
             c = pl.multiple_of(t * 256, 256)
-            first, second = None, None
-            for h in range(2):
-                d = h * HALF + col
-                rows_in = ring_in[s, 2 * h, :, col : col + width]
-                rows_grad = ring_in[s, 2 * h + 1, :, col : col + width]
-                one = dot_nn(rows_in, wi[pl.ds(d, width), pl.ds(c, 256)])
-                two = dot_nt(rows_grad, wo[pl.ds(c, 256), pl.ds(d, width)])
-                first = one if first is None else first + one
-                second = two if second is None else second + two
-            if col > 0:
-                first = first + acc[0, s, :, pl.ds(c, 256)]
-                second = second + acc[1, s, :, pl.ds(c, 256)]
-            if col + width == HALF:
-                pre_grad[s, :, pl.ds(c, 256)] = (second * gelu_slope(first)).astype(BF16)
+            sums = [None, None]
+            step = WIDE // width
+            for j in range(0, 4, step):
+                kind, d = blocks[j]
+                rows = [ring_in[s, j + i, :, col : col + width] for i in range(step)]
+                rows = rows[0] if step == 1 else jnp.concatenate(rows, axis=1)
+                if kind == 0:
+                    term = dot_nn(rows, wi[pl.ds(d, WIDE), pl.ds(c, 256)])
+                else:
+                    term = dot_nt(rows, wo[pl.ds(c, 256), pl.ds(d, WIDE)])
+                sums[kind] = term if sums[kind] is None else sums[kind] + term
+            here = pl.ds(c, 256)
+            if blocks is BLOCKS_A or blocks is BLOCKS_A1:
+                acc[0, s, :, here] = sums[0]
+            elif blocks is BLOCKS_A2:
+                acc[0, s, :, here] += sums[0]
+            elif blocks is BLOCKS_B:
+                acc[0, s, :, here] = gelu_slope(acc[0, s, :, here] + sums[0])
+                acc[1, s, :, here] = sums[1]
             else:
-                acc[0, s, :, pl.ds(c, 256)] = first
-                acc[1, s, :, pl.ds(c, 256)] = second
+                hidden_grad = acc[1, s, :, here] + sums[1]
+                pre_grad[s, :, here] = (hidden_grad * acc[0, s, :, here]).astype(BF16)
             return carry
 
         lax.fori_loop(0, 5, tile, 0)
@@ -360,7 +378,7 @@
             ).start()
             return carry
 
-        lax.fori_loop(1, RING, one, 0)
+        lax.fori_loop(0, RING - 1, one, 0)
         back_in[s, :, pl.ds(z * 16, 16), pl.ds(col, width)] = back_out[
             s, :, pl.ds(z * 16, 16), pl.ds(col, width)
         ]
@@ -381,7 +399,7 @@
             ).start()
             return carry
 
-        lax.fori_loop(1, PLANE, one, 0)
+        lax.fori_loop(0, PLANE - 1, one, 0)
         sig[s, pl.ds(pos * 8, 8), pl.ds(col, width)] = back_send[
             s, pl.ds(pos * 8, 8), pl.ds(col, width)
         ]
@@ -439,45 +457,52 @@
             ).start()
             return carry
 
-        lax.fori_loop(1, PLANE, one, 0)
+        lax.fori_loop(0, PLANE - 1, one, 0)
         dp_plane[s, pl.ds(pos * 8, 8)] = dp_sum[s, pl.ds(pos * 8, 8)]
 
-    def proj_ring(s):
+    def proj_pack(s):
         wait_bytes(dp_plane.at[s, pl.ds(0, 120)], dpr.at[s, 1])
-        dp_ring[s] = jnp.sum(dp_plane[s].reshape(PLANE, 8, 384), axis=0)
-
+        total = jnp.sum(dp_plane[s].reshape(PLANE, 8, 384), axis=0)
+        for k in range(3):
+            dp_pack[:, s * 3 + k, :] = total[:, k * 128 : k * 128 + 128]
+
+    def proj_ring():
         def one(q, carry):
             there, _, device = ring_peer(q)
             remote(
-                dp_ring.at[s], dp_back.at[s, pl.ds(z * 8, 8)],
-                dps.at[s, 2], dpr.at[s, 2], device,
-            ).start()
-            return carry
-
-        lax.fori_loop(1, RING, one, 0)
-        dp_back[s, pl.ds(z * 8, 8)] = dp_ring[s]
-
-    def proj_end(s):
-        wait_bytes(dp_back.at[s, pl.ds(0, 56)], dpr.at[s, 2])
-        total = jnp.sum(dp_back[s].reshape(RING, 8, 384), axis=0)
-        mine = jnp.sum(
-            jnp.where(iota2((8, 384), 0) == z, total, 0.0), axis=0, keepdims=True
-        )
-        dproj_ref[s : s + 1, :] = jnp.where(core == 0, mine[:, 0:320], mine[:, 64:384])
-
-    first_arrived()
-    for k in range(1, NF // 2 + 1):
-        ring_arrived(k)
-        expert(k - 1)
+                dp_pack.at[there], dp_back.at[z], dps.at[0, 2], dpr.at[0, 2], device
+            ).start()
+            return carry
+
+        lax.fori_loop(0, RING - 1, one, 0)
+        dp_back[z] = dp_pack[z]
+
+    def proj_end():
+        wait_bytes(dp_back.at[pl.ds(0, 7)], dpr.at[0, 2])
+        total = jnp.sum(dp_back[...], axis=0)
+        for s in range(2):
+            mine = jnp.concatenate([total[s * 3 + k : s * 3 + k + 1] for k in range(3)], axis=1)
+            dproj_ref[s : s + 1, :] = jnp.where(core == 0, mine[:, 0:320], mine[:, 64:384])
+
+    first_spread(1)
+    first_arrived(0)
+    expert(0)
+    ring_arrived(2)
+    first_arrived(1)
+    expert(2)
+    ring_arrived(3)
+    expert(1)
+    expert(3)
     for b in range(NB):
         expert_back(0, b)
     ring_arrived(4)
     for b in range(NB):
         back_ring(0, b)
-    expert(3)
+    expert(4)
     ring_arrived(5)
-    expert(4)
     expert(5)
+    ring_arrived(6)
+    expert(6)
     for b in range(NB):
         expert_back(1, b)
         if b > 0:
@@ -490,29 +515,32 @@
     arrived(0, 1)
     back_plane(1, 1)
     arrived(0, 2)
+    arrived(0, 3)
     back_plane(1, 2)
+    back_plane(1, 3)
     proj_start(0)
     arrived(1, 0)
     proj_plane(0)
     arrived(1, 1)
     arrived(1, 2)
+    arrived(1, 3)
     proj_start(1)
     proj_plane(1)
-    proj_ring(0)
+    proj_pack(0)
     whole = split(logit_grad[...])
     for c in range(0, D, 256):
         dacts[:, c : c + 256] = three(
             dot_nn, (disp_s[0], disp_s[1]), (grad_s[0, :, c : c + 256], grad_s[1, :, c : c + 256])
         ) + three(dot_nt, whole, (sp_s[0, c : c + 256, :], sp_s[1, c : c + 256, :]))
-    proj_ring(1)
-    proj_end(0)
-    proj_end(1)
+    proj_pack(1)
+    proj_ring()
+    proj_end()
 
     for k in range(NF):
-        s, col, width = FORWARD[k]
-        if k == 0:
-            wait_bytes(first_plane.at[:, pl.ds(0, 240)], fps.at[k])
-            wait_bytes(first_in.at[:, pl.ds(0, 112)], fzs.at[k])
+        s, col, width, blocks = FORWARD[k]
+        if k < 2:
+            wait_bytes(first_plane.at[k, :, pl.ds(0, 240), pl.ds(0, width)], fps.at[k])
+            wait_bytes(first_in.at[k, :, pl.ds(0, 112), pl.ds(0, width)], fzs.at[k])
         else:
             wait_bytes(plane_in.at[s, pl.ds(0, 240), pl.ds(col, width)], fps.at[k])
             wait_bytes(ring_in.at[s, :, pl.ds(0, 112), pl.ds(col, width)], fzs.at[k])
@@ -525,7 +553,7 @@
             wait_bytes(sig.at[s, pl.ds(0, 120), pl.ds(col, width)], bps.at[s, b])
         proj_across(s).wait_send()
         wait_bytes(dp_plane.at[s, pl.ds(0, 120)], dps.at[s, 1])
-        wait_bytes(dp_back.at[s, pl.ds(0, 56)], dps.at[s, 2])
+    wait_bytes(dp_back.at[pl.ds(0, 7)], dps.at[0, 2])
 
 
 def local(activations, out_grad, slot_out, slot_proj, w_in, w_out):
@@ -563,10 +591,10 @@
             vmem((2, ROWS, HALF), BF16),
             vmem((2, 16, 16, HALF), BF16),
             vmem((2, 4, ROWS, HALF), BF16),
-            vmem((16, 16, WIDE), BF16),
-            vmem((4, 128, WIDE), BF16),
-            vmem((2, ROWS, WIDE), BF16),
-            vmem((2, ROWS, WIDE), BF16),
+            vmem((2, 16, 16, WIDE), BF16),
+            vmem((2, 4, 128, WIDE), BF16),
+            vmem((2, 2, ROWS, WIDE), BF16),
+            vmem((2, 2, ROWS, WIDE), BF16),
             vmem((2, 2, ROWS, D), F32),
             vmem((2, ROWS, D), BF16),
             vmem((2, 2, ROWS, HALF), F32),
@@ -580,8 +608,8 @@
             vmem((2, SLOTS, 384), F32),
             vmem((2, SLOTS, 384), F32),
             vmem((2, SLOTS, 384), F32),
-            vmem((2, 8, 384), F32),
-            vmem((2, 64, 384), F32),
+            vmem((8, 8, 128), F32),
+            vmem((8, 8, 128), F32),
             sems((6,)),
             sems((NF,)), sems((NF,)), sems((NF,)), sems((NF,)), sems((NF,)), sems((NF,)),
             sems((2, NB)), sems((2, NB)), sems((2, NB)), sems((2, NB)), sems((2, NB)), sems((2, NB)),

time: 80.6 us -> 78.9 us (0.979)
  Pallas kernels: 78.2 us -> 76.5 us
    pallas_call x1, Pallas kernels: 78.2 us -> 76.5 us  [local(): pl.pallas_call(kernel, out_shape=(pltpu.VMEM((TOKENS, D), F32), pltpu.VME...]
where the time goes in v5:
time: 78.9 us; the launch traced here: 78.8 us
  Pallas kernels  76.5 us (97%)
  local copies, waits for them, and re-layouts  1.64 us (2%)
    pallas_call x1, Pallas kernels, local(): pl.pallas_call(kernel, out_shape=(pltpu.VMEM((TOKENS, D), F32), pltpu.VME...  76.5 us
    unnamed x2, local copies, waits for them, and re-layouts  1.64 us

profile of v5, /device:TPU:1, one launch (start us, length us, event | category | flops | bytes accessed | tf_op | source)
XLA Modules:
  0.0 78.8 jit_solution(13413108652357584521)
XLA Ops:
  0.6 76.5 %soft_moe_backward.1 = (f32[256,1280]{1,0:T(8,128)S(1)}, f32[2,320]{1,0:T(2,128)S(1)}) custom-call(f32[256,1280]{1,0:T(8,128)} %bitcast.11, f32[256,1280]{1,0:T(8,128)} %bitcast.12, f32[128,1280]{1,0:T(8,128)} %bitcast.13, f32[1280,128]{1,0:T(8,128)} %sp_hbm.1, bf16[1280,1280]{1,0:T(8,128)(2,1)} %bitcast.9, bf16[1280,1280]{1,0:T(8,128)(2,1)} %bitcast.10), custom_call_target="tpu_custom_call" | custom-call | tf_op jit(solution)/shard_map/soft_moe_backward/pallas_call | solution.py:563
  77.2 1.1 %copy.10 = f32[1,256,1280]{2,1,0:T(8,128)} copy(f32[1,256,1280]{2,1,0:T(8,128)S(1)} %bitcast.7) | data formatting | bytes 2621440
  78.2 0.6 copy.11

commit v6 on v5

--- a/solution.py
+++ b/solution.py
@@ -315,23 +315,25 @@
         wait_bytes(ring_in.at[s, :, pl.ds(0, 112), pl.ds(col, width)], fzr.at[k])
         across(k).start()
 
-    def expert(k):
-        s, col, width, blocks = FORWARD[k]
-        across(k).wait_recv()
-
-        def tile(t, carry):
-            c = pl.multiple_of(t * 256, 256)
+    def expert(k, begin=0, end=5):
+        s, col, width, blocks = FORWARD[k]
+        if begin == 0:
+            across(k).wait_recv()
+
+        def tile(t):
+            c = t * 256
             sums = [None, None]
-            step = WIDE // width
-            for j in range(0, 4, step):
-                kind, d = blocks[j]
-                rows = [ring_in[s, j + i, :, col : col + width] for i in range(step)]
-                rows = rows[0] if step == 1 else jnp.concatenate(rows, axis=1)
+            for kind in range(2):
+                which = [j for j in range(4) if blocks[j][0] == kind]
+                if not which:
+                    continue
+                rows = [ring_in[s, j, :, col : col + width] for j in which]
+                rows = rows[0] if len(rows) == 1 else jnp.concatenate(rows, axis=1)
+                span = pl.ds(blocks[which[0]][1], width * len(which))
                 if kind == 0:
-                    term = dot_nn(rows, wi[pl.ds(d, WIDE), pl.ds(c, 256)])
+                    sums[0] = dot_nn(rows, wi[span, pl.ds(c, 256)])
                 else:
-                    term = dot_nt(rows, wo[pl.ds(c, 256), pl.ds(d, WIDE)])
-                sums[kind] = term if sums[kind] is None else sums[kind] + term
+                    sums[1] = dot_nt(rows, wo[pl.ds(c, 256), span])
             here = pl.ds(c, 256)
             if blocks is BLOCKS_A or blocks is BLOCKS_A1:
                 acc[0, s, :, here] = sums[0]
@@ -343,9 +345,9 @@
             else:
                 hidden_grad = acc[1, s, :, here] + sums[1]
                 pre_grad[s, :, here] = (hidden_grad * acc[0, s, :, here]).astype(BF16)
-            return carry
-
-        lax.fori_loop(0, 5, tile, 0)
+
+        for t in range(begin, end):
+            tile(t)
 
     def back_across(s, b):
         col, width = BACK[b]
@@ -357,10 +359,14 @@
 
     def expert_back(s, b):
         col, width = BACK[b]
-        for h in range(2):
-            part[s, h, :, col : col + width] = dot_nt(
-                pre_grad[s], wi[h * HALF + col : h * HALF + col + width, :]
-            )
+        weights = [wi[h * HALF + col : h * HALF + col + width, :] for h in range(2)]
+        if width == 128:
+            rows = dot_nt(pre_grad[s], jnp.concatenate(weights, axis=0))
+            for h in range(2):
+                part[s, h, :, col : col + width] = rows[:, h * width : h * width + width]
+        else:
+            for h in range(2):
+                part[s, h, :, col : col + width] = dot_nt(pre_grad[s], weights[h])
         back_across(s, b).start()
 
     def back_ring(s, b):
@@ -486,22 +492,23 @@
 
     first_spread(1)
     first_arrived(0)
+    ring_arrived(2)
     expert(0)
-    ring_arrived(2)
     first_arrived(1)
+    ring_arrived(3)
     expert(2)
-    ring_arrived(3)
     expert(1)
     expert(3)
+    ring_arrived(4)
     for b in range(NB):
         expert_back(0, b)
-    ring_arrived(4)
+    expert(4)
+    ring_arrived(5)
     for b in range(NB):
         back_ring(0, b)
-    expert(4)
-    ring_arrived(5)
-    expert(5)
+    expert(5, 0, 3)
     ring_arrived(6)
+    expert(5, 3, 5)
     expert(6)
     for b in range(NB):
         expert_back(1, b)
@@ -511,13 +518,13 @@
     for b in range(NB):
         back_plane(0, b)
     back_plane(1, 0)
+    back_plane(1, 1)
     arrived(0, 0)
     arrived(0, 1)
-    back_plane(1, 1)
+    back_plane(1, 2)
     arrived(0, 2)
+    back_plane(1, 3)
     arrived(0, 3)
-    back_plane(1, 2)
-    back_plane(1, 3)
     proj_start(0)
     arrived(1, 0)
     proj_plane(0)
@@ -554,6 +561,17 @@
         proj_across(s).wait_send()
         wait_bytes(dp_plane.at[s, pl.ds(0, 120)], dps.at[s, 1])
     wait_bytes(dp_back.at[pl.ds(0, 7)], dps.at[0, 2])
+
+
+def deliver(dacts, dproj, dacts_hbm, dproj_hbm, sem):
+    copies = [
+        pltpu.make_async_copy(dacts, dacts_hbm, sem.at[0]),
+        pltpu.make_async_copy(dproj, dproj_hbm, sem.at[1]),
+    ]
+    for copy in copies:
+        copy.start()
+    for copy in copies:
+        copy.wait()
 
 
 def local(activations, out_grad, slot_out, slot_proj, w_in, w_out):
@@ -620,6 +638,18 @@
         ),
         name="soft_moe_backward",
     )(activations[0], out_grad[0], slot_out[0], slot_proj, w_in[0], w_out[0])
+    d_acts, d_proj = pl.pallas_call(
+        deliver,
+        out_shape=(
+            jax.ShapeDtypeStruct((TOKENS, D), F32),
+            jax.ShapeDtypeStruct((2, 320), F32),
+        ),
+        in_specs=[pl.BlockSpec(memory_space=pltpu.VMEM)] * 2,
+        out_specs=(any_space,) * 2,
+        scratch_shapes=[sems((2,))],
+        compiler_params=pltpu.CompilerParams(vmem_limit_bytes=2**20),
+        name="deliver",
+    )(d_acts, d_proj)
     return d_acts[None], d_proj.T
 
 

time: 78.9 us -> 76.3 us (0.967)
  local copies, waits for them, and re-layouts: 1.64 us -> 0 us
  Pallas kernels: 76.5 us -> 75.5 us
    pallas_call x1, Pallas kernels: 76.5 us -> 74.4 us  [local(): pl.pallas_call(kernel, out_shape=(pltpu.VMEM((TOKENS, D), F32), pltpu.VME...]
    unnamed x2 -> x0, local copies, waits for them, and re-layouts: 1.64 us -> none
    pallas_call x0 -> x1, Pallas kernels: none -> 1.08 us  [local(): pl.pallas_call(deliver, out_shape=(jax.ShapeDtypeStruct((TOKENS, D), F32)...]
where the time goes in v6:
time: 76.3 us
  Pallas kernels  75.5 us (99%)
  between operations  0.8 us (1%)
    pallas_call x1, Pallas kernels, local(): pl.pallas_call(kernel, out_shape=(pltpu.VMEM((TOKENS, D), F32), pltpu.VME...  74.4 us

profile of v6, /device:TPU:1, one launch (start us, length us, event | category | flops | bytes accessed | tf_op | source)
XLA Modules:
  0.0 76.3 jit_solution(16221592773971527475)
XLA Ops:
  0.6 74.4 %soft_moe_backward.1 = (f32[256,1280]{1,0:T(8,128)S(1)}, f32[2,320]{1,0:T(2,128)S(1)}) custom-call(f32[256,1280]{1,0:T(8,128)} %bitcast.9, f32[256,1280]{1,0:T(8,128)} %bitcast.10, f32[128,1280]{1,0:T(8,128)} %bitcast.11, f32[1280,128]{1,0:T(8,128)} %sp_hbm.1, bf16[1280,1280]{1,0:T(8,128)(2,1)} %bitcast.7, bf16[1280,1280]{1,0:T(8,128)(2,1)} %bitcast.8), custom_call_target="tpu_custom_call" | custom-call | tf_op jit(solution)/shard_map/soft_moe_backward/pallas_call | solution.py:581
  75.0 1.1 %deliver.1 = (f32[256,1280]{1,0:T(8,128)}, f32[2,320]{1,0:T(2,128)}) custom-call(f32[256,1280]{1,0:T(8,128)S(1)} %get-tuple-element.6.dacts, f32[2,320]{1,0:T(2,128)S(1)} %get-tuple-element.7.dproj), custom_call_target="tpu_custom_call" | custom-call | tf_op jit(solution)/shard_map/deliver/pallas_call | solution.py:641

commit v7 on v6

--- a/solution.py
+++ b/solution.py
@@ -19,14 +19,12 @@
 RING = 8
 WIDE = 256
 BLOCKS_A = ((0, 0), (0, 256), (0, 512), (0, 768))
-BLOCKS_A1 = ((0, 0), (0, 128), (0, 256), (0, 384))
-BLOCKS_A2 = ((0, 512), (0, 640), (0, 768), (0, 896))
 BLOCKS_B = ((0, 1024), (1, 0), (1, 256), (1, 512))
 BLOCKS_C = ((1, 768), (1, 896), (1, 1024), (1, 1152))
 FORWARD = (
-    (0, 0, 256, BLOCKS_A), (1, 0, 128, BLOCKS_A1),
+    (0, 0, 256, BLOCKS_A), (1, 0, 256, BLOCKS_A),
     (0, 256, 256, BLOCKS_B), (0, 512, 128, BLOCKS_C),
-    (1, 128, 128, BLOCKS_A2), (1, 256, 256, BLOCKS_B), (1, 512, 128, BLOCKS_C),
+    (1, 256, 256, BLOCKS_B), (1, 512, 128, BLOCKS_C),
 )
 BACK = ((0, 128), (128, 256), (384, 128), (512, 128))
 NF, NB = len(FORWARD), len(BACK)
@@ -104,7 +102,7 @@
     pairs = ((sp_hbm, sp), (acts_hbm, acts), (og_hbm, og), (so_hbm, so), (wi_hbm, wi), (wo_hbm, wo))
     for k, (src, dst) in enumerate(pairs):
         loads.append(pltpu.make_async_copy(src, dst, load_sem.at[k]))
-        if k < 3:
+        if k < 2:
             loads[-1].start()
     load_sp, load_acts, load_og, load_so, load_wi, load_wo = loads
 
@@ -118,8 +116,8 @@
         pl.semaphore_signal(barrier, inc=1, device_id=ring_peer(q)[2], device_id_type=MESH)
         return carry
 
+    lax.fori_loop(0, RING - 1, greet_ring, 0)
     lax.fori_loop(0, PLANE - 1, greet_plane, 0)
-    lax.fori_loop(0, RING - 1, greet_ring, 0)
     pl.semaphore_signal(barrier, inc=1, device_id=other, device_id_type=MESH)
 
     n, r = iota2((SLOTS, SLOTS), 0), iota2((SLOTS, SLOTS), 1)
@@ -155,8 +153,8 @@
     def twice(s):
         return one_hot(r == s * 64 + lax.div(n, 8) * 4 + lax.rem(n, 4))
 
-    dp_pack[...] = jnp.zeros_like(dp_pack)
     load_sp.wait()
+    load_og.start()
     for k, part_of in enumerate(split(sp[...])):
         sp_s[k] = dot_nn(part_of, to_order).astype(BF16)
     load_acts.wait()
@@ -298,6 +296,7 @@
     for k in range(3, NF):
         ring_send(k)
 
+    dp_pack[...] = jnp.zeros_like(dp_pack)
     load_so.wait()
     for k, part_of in enumerate(split(so[...])):
         so_s[k] = dot_nn(to_order_t, part_of).astype(BF16)
@@ -335,10 +334,8 @@
                 else:
                     sums[1] = dot_nt(rows, wo[pl.ds(c, 256), span])
             here = pl.ds(c, 256)
-            if blocks is BLOCKS_A or blocks is BLOCKS_A1:
+            if blocks is BLOCKS_A:
                 acc[0, s, :, here] = sums[0]
-            elif blocks is BLOCKS_A2:
-                acc[0, s, :, here] += sums[0]
             elif blocks is BLOCKS_B:
                 acc[0, s, :, here] = gelu_slope(acc[0, s, :, here] + sums[0])
                 acc[1, s, :, here] = sums[1]
@@ -437,7 +434,7 @@
             grad - jnp.sum(grad * dispatch, axis=0, keepdims=True)
         )
         logit_grad[...] = whole
-        rows = [dot_nn(twice(s), a).astype(BF16) for a in split(whole.T)]
+        rows = [dot_nt(twice(s), a).astype(BF16) for a in split(whole)]
         upper = lax.rem(lax.div(iota2((SLOTS, 384), 0), 4), 2) == 0
 
         def half(which):
@@ -492,24 +489,22 @@
 
     first_spread(1)
     first_arrived(0)
+    expert(0)
     ring_arrived(2)
-    expert(0)
     first_arrived(1)
+    expert(2)
     ring_arrived(3)
-    expert(2)
     expert(1)
     expert(3)
+    for b in range(NB):
+        expert_back(0, b)
     ring_arrived(4)
     for b in range(NB):
-        expert_back(0, b)
-    expert(4)
+        back_ring(0, b)
+    expert(4, 0, 3)
     ring_arrived(5)
-    for b in range(NB):
-        back_ring(0, b)
-    expert(5, 0, 3)
-    ring_arrived(6)
-    expert(5, 3, 5)
-    expert(6)
+    expert(4, 3, 5)
+    expert(5)
     for b in range(NB):
         expert_back(1, b)
         if b > 0:

time: 76.3 us -> 76.1 us (level)
  no operation moved by 1% of the time
where the time goes in v7:
time: 76.1 us; the launch traced here: 76 us
  Pallas kernels  75.2 us (99%)
  between operations  0.8 us (1%)
    pallas_call x1, Pallas kernels, local(): pl.pallas_call(kernel, out_shape=(pltpu.VMEM((TOKENS, D), F32), pltpu.VME...  74.1 us

profile of v7, /device:TPU:1, one launch (start us, length us, event | category | flops | bytes accessed | tf_op | source)
XLA Modules:
  0.0 76.0 jit_solution(1208177307869640884)
XLA Ops:
  0.6 74.1 %soft_moe_backward.1 = (f32[256,1280]{1,0:T(8,128)S(1)}, f32[2,320]{1,0:T(2,128)S(1)}) custom-call(f32[256,1280]{1,0:T(8,128)} %bitcast.9, f32[256,1280]{1,0:T(8,128)} %bitcast.10, f32[128,1280]{1,0:T(8,128)} %bitcast.11, f32[1280,128]{1,0:T(8,128)} %sp_hbm.1, bf16[1280,1280]{1,0:T(8,128)(2,1)} %bitcast.7, bf16[1280,1280]{1,0:T(8,128)(2,1)} %bitcast.8), custom_call_target="tpu_custom_call" | custom-call | tf_op jit(solution)/shard_map/soft_moe_backward/pallas_call | solution.py:576
  74.7 1.1 %deliver.1 = (f32[256,1280]{1,0:T(8,128)}, f32[2,320]{1,0:T(2,128)}) custom-call(f32[256,1280]{1,0:T(8,128)S(1)} %get-tuple-element.6.dacts, f32[2,320]{1,0:T(2,128)S(1)} %get-tuple-element.7.dproj), custom_call_target="tpu_custom_call" | custom-call | tf_op jit(solution)/shard_map/deliver/pallas_call | solution.py:636
